TPU v7x, 32 devices: a whole 2x2x4 slice. The times are simulated.
32 devices in a mesh: camp: 4 (over y, core), hour: 8 (over z, x).
Axes of the slice: x: 2, y: 2, z: 4, core: 2. Of those that a mesh axis runs over, the one named last changes fastest.
Arguments:
- observed: bfloat16 [512, 1024, 128], P('camp', 'hour'), may hold values from -6 to 6
- bucket: int32 [512, 1024, 128], P('camp', 'hour'), may hold values from 0 to 8
- propensity: float32 [8], replicated, may hold values from 0.1 to 1
- camp_factor: float32 [512, 256], P(('camp', 'hour')), may hold values from -2.4 to 2.4
- camp_moment: float32 [512, 256], P(('camp', 'hour')), may hold values from -0.6 to 0.6
- camp_second: float32 [512, 256], P(('camp', 'hour')), may hold values from 0.02 to 0.5
- hour_factor: float32 [1024, 256], P(('hour', 'camp')), may hold values from -2.4 to 2.4
- hour_moment: float32 [1024, 256], P(('hour', 'camp')), may hold values from -0.6 to 0.6
- hour_second: float32 [1024, 256], P(('hour', 'camp')), may hold values from 0.02 to 0.5
- delay_factor: float32 [128, 256], replicated, may hold values from -2.4 to 2.4
- delay_moment: float32 [128, 256], replicated, may hold values from -0.6 to 0.6
- delay_second: float32 [128, 256], replicated, may hold values from 0.02 to 0.5
Outputs:
- new_camp: float32 [512, 256], P(('camp', 'hour'))
- new_hour: float32 [1024, 256], P(('hour', 'camp'))
- new_delay: float32 [128, 256], replicated
Inputs may be any that keep to these rules, and one draw needn't show every extreme that they name: 0 marks a censored entry; bucket b of 1 to 8 takes propensity entry b - 1.
All inputs are finite; a program needn't handle non-finite values.
Results may differ from a plain program's by a relative error of at most 0.01.
Values may be sent and summed in bfloat16 or wider, within the bound.
No kernel may reach another device: no remote copies, remote signals or barrier semaphores. Data moves between devices by JAX's collectives and lax.ppermute only.
A program may use at most 128 MiB of HBM per device.

v0:
```python
import math

import jax
import jax.numpy as jnp
from jax import lax
from jax.sharding import PartitionSpec as P

STEPS = 2


learn_rate = 0.1
beta_first = 0.9
beta_second = 0.999
adam_eps = 1e-08


def adam_update(factor, moment, second, gradient, grad_scale):
    scaled = gradient * grad_scale
    moment = beta_first * moment + (1.0 - beta_first) * scaled
    second = beta_second * second + (1.0 - beta_second) * scaled * scaled
    factor = factor - learn_rate * moment / (jnp.sqrt(second) + adam_eps)
    return (factor, moment, second)


def entry_weights(bucket, propensity):
    inverse = 1.0 / propensity
    weight = jnp.zeros(bucket.shape, jnp.float32)
    for bucket_level in range(propensity.shape[0]):
        weight = weight + jnp.where(
            bucket == bucket_level + 1, inverse[bucket_level], jnp.float32(0.0)
        )
    return weight


def local_terms(observed, weight, camp_block, hour_block, delay_block):
    tile_rows, tile_cols, delay_count = observed.shape
    rank_width = camp_block.shape[1]
    khatri = (
        hour_block.astype(jnp.float32)[:, None, :] * delay_block.astype(jnp.float32)[None, :, :]
    ).astype(jnp.bfloat16)
    khatri = khatri.reshape(tile_cols * delay_count, rank_width)
    model_tile = lax.dot_general(
        camp_block, khatri, (((1,), (1,)), ((), ())), preferred_element_type=jnp.float32
    )
    flat_obs = observed.reshape(tile_rows, tile_cols * delay_count).astype(jnp.float32)
    flat_weight = weight.reshape(tile_rows, tile_cols * delay_count)
    residual = (flat_weight * (model_tile - flat_obs)).astype(jnp.bfloat16)
    spread = lax.dot_general(
        residual, camp_block, (((0,), (0,)), ((), ())), preferred_element_type=jnp.float32
    )
    spread = spread.reshape(tile_cols, delay_count, rank_width)
    hour_grad = jnp.sum(spread * delay_block.astype(jnp.float32)[None, :, :], axis=1)
    delay_grad = jnp.sum(spread * hour_block.astype(jnp.float32)[:, None, :], axis=0)
    return (khatri, residual, hour_grad, delay_grad)


def body(
    observed,
    bucket,
    propensity,
    camp_factor,
    camp_moment,
    camp_second,
    hour_factor,
    hour_moment,
    hour_second,
    delay_factor,
    delay_moment,
    delay_second,
):
    tile_rows, tile_cols, delay_count = observed.shape
    camp_count = lax.axis_size("camp")
    hour_count = lax.axis_size("hour")
    campaigns = tile_rows * camp_count
    total_hours = tile_cols * hour_count
    camp_scale = 1.0 / math.sqrt(total_hours * delay_count)
    hour_scale = 1.0 / math.sqrt(campaigns * delay_count)
    delay_scale = 1.0 / math.sqrt(campaigns * total_hours)
    weight = entry_weights(bucket, propensity)
    for iteration in range(STEPS):
        camp_block = lax.all_gather(camp_factor.astype(jnp.bfloat16), "hour", axis=0, tiled=True)
        hour_block = lax.all_gather(hour_factor.astype(jnp.bfloat16), "camp", axis=0, tiled=True)
        delay_block = delay_factor.astype(jnp.bfloat16)
        khatri, residual, hour_grad, delay_grad = local_terms(
            observed, weight, camp_block, hour_block, delay_block
        )
        camp_grad = lax.psum_scatter(
            jnp.dot(residual, khatri, preferred_element_type=jnp.float32).astype(jnp.bfloat16),
            "hour",
            scatter_dimension=0,
            tiled=True,
        ).astype(jnp.float32)
        hour_grad = lax.psum_scatter(
            hour_grad.astype(jnp.bfloat16), "camp", scatter_dimension=0, tiled=True
        ).astype(jnp.float32)
        camp_factor, camp_moment, camp_second = adam_update(
            camp_factor, camp_moment, camp_second, camp_grad, camp_scale
        )
        hour_factor, hour_moment, hour_second = adam_update(
            hour_factor, hour_moment, hour_second, hour_grad, hour_scale
        )
        delay_grad = lax.psum(delay_grad, ("camp", "hour"))
        delay_factor, delay_moment, delay_second = adam_update(
            delay_factor, delay_moment, delay_second, delay_grad, delay_scale
        )
    return (camp_factor, hour_factor, delay_factor)


def solution(mesh):
    in_specs = (
        P("camp", "hour", None),
        P("camp", "hour", None),
        P(),
        P(("camp", "hour"), None),
        P(("camp", "hour"), None),
        P(("camp", "hour"), None),
        P(("hour", "camp"), None),
        P(("hour", "camp"), None),
        P(("hour", "camp"), None),
        P(),
        P(),
        P(),
    )
    out_specs = (P(("camp", "hour"), None), P(("hour", "camp"), None), P())
    return jax.shard_map(body, mesh=mesh, in_specs=in_specs, out_specs=out_specs, check_vma=False)
```

profile of v0, /device:TPU:0, one launch (start us, length us, event | category | flops | bytes accessed | tf_op | source)
XLA Modules:
  0.0 441.1 jit_solution(12552705200140923853)
XLA Ops:
  8.0 0.7 broadcast_divide_fusion
  8.7 0.7 fusion.29
  9.4 0.7 convert_element_type.91
  10.1 0.8 convert_element_type.85
  10.8 6.2 %all_gather.12 = bf16[128,256]{1,0:T(8,128)(2,1)S(1)} all-gather(bf16[32,256]{1,0:T(8,128)(2,1)S(1)} %convert_element_type.85), channel_id=1, replica_groups=mesh['camp'=4,'hour'=8] {'camp'}, dimensions={0}, use_global_device_ids=true | all-gather | bytes 81920 | tf_op jit(solution)/shard_map/all_gather | solution.py:82
  17.0 31.3 %all_gather.13 = bf16[128,256]{1,0:T(8,128)(2,1)S(1)} all-gather(bf16[16,256]{1,0:T(8,128)(2,1)S(1)} %convert_element_type.91), channel_id=1, replica_groups=mesh['camp'=4,'hour'=8] {'hour'}, dimensions={0}, use_global_device_ids=true | all-gather | bytes 73728 | tf_op jit(solution)/shard_map/all_gather | solution.py:81
  48.4 0.9 convert_convert_fusion.1
  49.3 15.4 %select_add_fusion = f32[128,128,128]{2,1,0:T(8,128)} fusion(s32[128,128,128]{2,1,0:T(8,128)} %param.13, f32[]{:T(128)} %bitcast.7, f32[]{:T(128)} %bitcast.6, f32[]{:T(128)} %bitcast.5, f32[]{:T(128)} %bitcast.4, f32[]{:T(128)} %bitcast.3, f32[]{:T(128)} %bitcast.2, f32[]{:T(128)} %bitcast.1, f32[]{:T(128)} %bitcast), kind=kLoop, calls=%fused_computation.13 | loop fusion | flops 48234496 | bytes 16777248 | tf_op jit(solution)/shard_map/add | solution.py:29
  64.7 9.3 %copy.15 = f32[128,128,128]{0,2,1:T(8,128)} copy(f32[128,128,128]{2,1,0:T(8,128)} %select_add_fusion) | data formatting | bytes 16777216 | tf_op jit(solution)/shard_map/add | solution.py:29
  74.1 7.6 %copy.16 = f32[128,128,128]{0,2,1:T(8,128)} copy(bf16[128,128,128]{2,1,0:T(8,128)(2,1)} %param.12) | data formatting | bytes 12582912 | tf_op jit(solution)/shard_map/convert_element_type | solution.py:45
  81.7 3.5 multiply_convert_fusion.1
  85.2 11.3 %fusion.3 = bf16[128,16384]{0,1:T(8,128)(2,1)S(1)} fusion(f32[128,16384]{0,1:T(8,128)} %bitcast.40, f32[128,16384]{0,1:T(8,128)} %bitcast.42, bf16[16384,256]{1,0:T(8,128)(2,1)S(1)} %bitcast.38, bf16[128,256]{1,0:T(8,128)(2,1)S(1)} %all_gather.13), kind=kOutput, calls=%fused_computation.5 | convolution fusion | flops 1080033280 | bytes 29425664 | tf_op jit(solution)/shard_map/dot_general | solution.py:42
  96.6 8.7 %multiply_reduce_fusion.3 = (bf16[128,256]{1,0:T(8,128)(2,1)}, f32[16384,256]{1,0:T(8,128)}) fusion(f32[128,256]{1,0:T(8,128)S(1)} %convert_convert_fusion.1, bf16[128,16384]{0,1:T(8,128)(2,1)S(1)} %fusion.3, bf16[128,256]{1,0:T(8,128)(2,1)S(1)} %all_gather.13), kind=kOutput, calls=%fused_computation.11 | convolution fusion | flops 1082097664 | bytes 21233664 | tf_op jit(solution)/shard_map/dot_general | solution.py:48
  105.3 8.3 %multiply_reduce_fusion.2 = f32[128,256]{1,0:T(8,128)} fusion(f32[128,128,256]{2,1,0:T(8,128)} %bitcast.44, f32[128,256]{1,0:T(8,128)S(1)} %convert_element_type.86), kind=kLoop, calls=%fused_computation.10 | loop fusion | flops 8355840 | bytes 17039360 | tf_op jit(solution)/shard_map/reduce_sum | solution.py:53
  113.7 7.2 %convolution_convert_fusion.1 = bf16[128,256]{1,0:T(8,128)(2,1)} fusion(bf16[128,16384]{0,1:T(8,128)(2,1)} %copy-done.3, bf16[16384,256]{1,0:T(8,128)(2,1)} %bitcast.39), kind=kOutput, calls=%fused_computation.15 | convolution fusion | flops 1073774592 | bytes 12648448 | tf_op jit(solution)/shard_map/dot_general | solution.py:88
  121.0 0.5 reduce-scatter.7.cloned.1.call-update
  121.6 115.5 %all-reduce.3.cloned.1.call-done = f32[128,256]{1,0:T(8,128)} async-done(((f32[128,256]{1,0:T(8,128)}), f32[128,256]{1,0:T(8,128)}) %all-reduce.3.cloned.1.call-update) | async-done | bytes 131088 | tf_op jit(solution)/shard_map/psum | solution.py:102
  237.1 1.0 convert_convert_fusion
  238.2 0.7 fusion.27
  238.9 30.5 %all_gather.14 = bf16[128,256]{1,0:T(8,128)(2,1)S(1)} all-gather(bf16[16,256]{1,0:T(8,128)(2,1)S(1)} %fusion.27), channel_id=1, replica_groups=mesh['camp'=4,'hour'=8] {'hour'}, dimensions={0}, use_global_device_ids=true | all-gather | bytes 73728 | tf_op jit(solution)/shard_map/all_gather | solution.py:81
  269.4 0.8 fusion.28
  270.2 5.5 %all_gather.15 = bf16[128,256]{1,0:T(8,128)(2,1)S(1)} all-gather(bf16[32,256]{1,0:T(8,128)(2,1)S(1)} %fusion.28), channel_id=1, replica_groups=mesh['camp'=4,'hour'=8] {'camp'}, dimensions={0}, use_global_device_ids=true | all-gather | bytes 81920 | tf_op jit(solution)/shard_map/all_gather | solution.py:82
  275.7 3.5 multiply_convert_fusion
  279.2 11.1 %fusion.4 = bf16[128,16384]{0,1:T(8,128)(2,1)S(1)} fusion(f32[128,16384]{0,1:T(8,128)} %bitcast.41, f32[128,16384]{0,1:T(8,128)} %bitcast.43, bf16[128,256]{1,0:T(8,128)(2,1)S(1)} %all_gather.14, bf16[16384,256]{1,0:T(8,128)(2,1)S(1)} %bitcast.36), kind=kOutput, calls=%fused_computation.6 | convolution fusion | flops 1080033280 | bytes 29425664 | tf_op jit(solution)/shard_map/dot_general | solution.py:42
  290.3 8.7 %multiply_reduce_fusion.1 = (bf16[128,256]{1,0:T(8,128)(2,1)}, f32[16384,256]{1,0:T(8,128)}) fusion(f32[128,256]{1,0:T(8,128)S(1)} %convert_convert_fusion, bf16[128,16384]{0,1:T(8,128)(2,1)S(1)} %fusion.4, bf16[128,256]{1,0:T(8,128)(2,1)S(1)} %all_gather.14), kind=kOutput, calls=%fused_computation.8 | convolution fusion | flops 1082097664 | bytes 21233664 | tf_op jit(solution)/shard_map/dot_general | solution.py:48
  299.0 8.3 %multiply_reduce_fusion = f32[128,256]{1,0:T(8,128)} fusion(f32[128,128,256]{2,1,0:T(8,128)} %bitcast.45, f32[128,256]{1,0:T(8,128)S(1)} %convert_element_type.101), kind=kLoop, calls=%fused_computation.7 | loop fusion | flops 8355840 | bytes 17039360 | tf_op jit(solution)/shard_map/reduce_sum | solution.py:53
  307.4 7.1 %convolution_convert_fusion = bf16[128,256]{1,0:T(8,128)(2,1)} fusion(bf16[128,16384]{0,1:T(8,128)(2,1)} %copy-done.2, bf16[16384,256]{1,0:T(8,128)(2,1)} %bitcast.37), kind=kOutput, calls=%fused_computation.14 | convolution fusion | flops 1073774592 | bytes 12648448 | tf_op jit(solution)/shard_map/dot_general | solution.py:88
  314.6 0.7 reduce-scatter.11.cloned.1.call-update
  315.3 113.8 %all-reduce.5.cloned.1.call-done = f32[128,256]{1,0:T(8,128)} async-done(((f32[128,256]{1,0:T(8,128)}), f32[128,256]{1,0:T(8,128)}) %all-reduce.5.cloned.1.call-update) | async-done | bytes 131088 | tf_op jit(solution)/shard_map/psum | solution.py:102
  429.1 1.7 divide_subtract_fusion
  430.8 1.3 fusion.22
  432.1 1.4 fusion.11
  (48 shorter events, 0.5 us)
Async XLA Ops:
  8.0 229.1 %all-reduce.3.cloned.1.call-start = ((), (), s32[]{:S(2)}) async-start(), calls=%async_computation.6 | async-start | bytes 262144 | tf_op jit(solution)/shard_map/psum | solution.py:102
  85.2 11.3 %copy-start.1 = (bf16[128,128,256]{2,1,0:T(8,128)(2,1)}, bf16[128,128,256]{2,1,0:T(8,128)(2,1)S(1)}, u32[]{:S(2)}) copy-start(bf16[128,128,256]{2,1,0:T(8,128)(2,1)S(1)} %multiply_convert_fusion.1) | copy-start | bytes 25165828
  96.6 8.7 %copy-start.3 = (bf16[128,16384]{0,1:T(8,128)(2,1)}, bf16[128,16384]{0,1:T(8,128)(2,1)S(1)}, u32[]{:S(2)}) copy-start(bf16[128,16384]{0,1:T(8,128)(2,1)S(1)} %fusion.3) | copy-start | bytes 12582916
  113.6 123.5 %copy-start.4 = (f32[128,256]{1,0:T(8,128)S(1)}, f32[128,256]{1,0:T(8,128)}, u32[]{:S(2)}) copy-start(f32[128,256]{1,0:T(8,128)} %param.21) | copy-start | bytes 393220
  113.6 123.5 %copy-start.5 = (f32[128,256]{1,0:T(8,128)S(1)}, f32[128,256]{1,0:T(8,128)}, u32[]{:S(2)}) copy-start(f32[128,256]{1,0:T(8,128)} %param.23) | copy-start | bytes 393220
  113.6 123.5 %copy-start.6 = (f32[128,256]{1,0:T(8,128)S(1)}, f32[128,256]{1,0:T(8,128)}, u32[]{:S(2)}) copy-start(f32[128,256]{1,0:T(8,128)} %param.22) | copy-start | bytes 393220
  113.6 124.6 %copy-start.9 = (f32[16,256]{1,0:T(8,128)S(1)}, f32[16,256]{1,0:T(8,128)}, u32[]{:S(2)}) copy-start(f32[16,256]{1,0:T(8,128)} %param.15) | copy-start | bytes 49156
  113.6 124.6 %copy-start.12 = (f32[16,256]{1,0:T(8,128)S(1)}, f32[16,256]{1,0:T(8,128)}, u32[]{:S(2)}) copy-start(f32[16,256]{1,0:T(8,128)} %param.17) | copy-start | bytes 49156
  113.6 124.5 %copy-start.13 = (f32[16,256]{1,0:T(8,128)S(1)}, f32[16,256]{1,0:T(8,128)}, u32[]{:S(2)}) copy-start(f32[16,256]{1,0:T(8,128)} %param.16) | copy-start | bytes 49156
  113.6 155.8 %copy-start.8 = (f32[32,256]{1,0:T(8,128)S(1)}, f32[32,256]{1,0:T(8,128)}, u32[]{:S(2)}) copy-start(f32[32,256]{1,0:T(8,128)} %param.18) | copy-start | bytes 98308
  113.7 155.8 %copy-start.10 = (f32[32,256]{1,0:T(8,128)S(1)}, f32[32,256]{1,0:T(8,128)}, u32[]{:S(2)}) copy-start(f32[32,256]{1,0:T(8,128)} %param.20) | copy-start | bytes 98308
  113.7 155.8 %copy-start.11 = (f32[32,256]{1,0:T(8,128)S(1)}, f32[32,256]{1,0:T(8,128)}, u32[]{:S(2)}) copy-start(f32[32,256]{1,0:T(8,128)} %param.19) | copy-start | bytes 98308
  113.7 124.5 %reduce-scatter.5.cloned.1.call-start = ((), (), s32[]{:S(2)}) async-start(), calls=%async_computation.4 | async-start | bytes 73728 | tf_op jit(solution)/shard_map/reduce_scatter | solution.py:87
  120.9 148.5 %reduce-scatter.7.cloned.1.call-start = ((), (), s32[]{:S(2)}) async-start(), calls=%async_computation.5 | async-start | bytes 81920 | tf_op jit(solution)/shard_map/reduce_scatter | solution.py:93
  121.5 307.5 %all-reduce.5.cloned.1.call-start = ((), (), s32[]{:S(2)}) async-start(), calls=%async_computation.9 | async-start | bytes 262144 | tf_op jit(solution)/shard_map/psum | solution.py:102
  279.2 11.2 %copy-start = (bf16[128,128,256]{2,1,0:T(8,128)(2,1)}, bf16[128,128,256]{2,1,0:T(8,128)(2,1)S(1)}, u32[]{:S(2)}) copy-start(bf16[128,128,256]{2,1,0:T(8,128)(2,1)S(1)} %multiply_convert_fusion) | copy-start | bytes 25165828
  290.3 8.7 %copy-start.2 = (bf16[128,16384]{0,1:T(8,128)(2,1)}, bf16[128,16384]{0,1:T(8,128)(2,1)S(1)}, u32[]{:S(2)}) copy-start(bf16[128,16384]{0,1:T(8,128)(2,1)S(1)} %fusion.4) | copy-start | bytes 12582916
  307.3 121.7 %copy-start.7 = (f32[128,256]{1,0:T(8,128)S(1)}, f32[128,256]{1,0:T(8,128)}, u32[]{:S(2)}) copy-start(f32[128,256]{1,0:T(8,128)} %all-reduce.3.cloned.1.call-done) | copy-start | bytes 393220
  307.3 123.5 %copy-start.15 = (bf16[16,256]{1,0:T(8,128)(2,1)S(1)}, bf16[16,256]{1,0:T(8,128)(2,1)}, u32[]{:S(2)}) copy-start(bf16[16,256]{1,0:T(8,128)(2,1)} %reduce-scatter.5.cloned.1.call-done) | copy-start | bytes 24580
  307.4 124.8 %copy-start.14 = (bf16[32,256]{1,0:T(8,128)(2,1)S(1)}, bf16[32,256]{1,0:T(8,128)(2,1)}, u32[]{:S(2)}) copy-start(bf16[32,256]{1,0:T(8,128)(2,1)} %reduce-scatter.7.cloned.1.call-done) | copy-start | bytes 49156
  307.4 123.4 %reduce-scatter.9.cloned.1.call-start = ((), (), s32[]{:S(2)}) async-start(), calls=%async_computation.7 | async-start | bytes 73728 | tf_op jit(solution)/shard_map/reduce_scatter | solution.py:87
  314.5 117.6 %reduce-scatter.11.cloned.1.call-start = ((), (), s32[]{:S(2)}) async-start(), calls=%async_computation.8 | async-start | bytes 81920 | tf_op jit(solution)/shard_map/reduce_scatter | solution.py:93
Sparse Core Ops, SparseCore 0:
  113.7 123.3 all-reduce.2
  307.5 121.5 all-reduce.4
Sparse Core Ops, SparseCore 1:
  121.0 62.4 reduce-scatter.4
  185.7 18.5 reduce-scatter.6
  314.6 60.4 reduce-scatter.8
  377.6 18.5 reduce-scatter.10
where the time goes:
time: 442 us; the launch traced here: 441 us
  waiting for transfers between devices  231 us (52%)
  blocking collectives  73.5 us (17%)
  matrix products  54.1 us (12%)
  other arithmetic  49 us (11%)
  local copies, waits for them, and re-layouts  17.7 us (4%)
  between operations  15.9 us (4%)
    psum x2, waiting for transfers between devices, body(): delay_grad = lax.psum(delay_grad, ('camp', 'hour'))  229 us
    all_gather x2, blocking collectives, body(): lax.all_gather(camp_factor.astype(jnp.bfloat16), 'hour', axis=0, tiled=True)  61.8 us
    dot_general x2, matrix products, local_terms(): lax.dot_general(camp_block, khatri, (((1,), (1,)), ((), ())), preferred_e...  22.5 us
    dot_general x2, matrix products, local_terms(): lax.dot_general(residual, camp_block, (((0,), (0,)), ((), ())), preferred...  17.4 us
    reduce_sum x2, other arithmetic, local_terms(): jnp.sum(spread * hour_block.astype(jnp.float32)[:, None, :], axis=0)  16.6 us
    add x1, other arithmetic, entry_weights(): weight + jnp.where(bucket == bucket_level + 1, inverse[bucket_level], jnp...  15.4 us
    dot_general x2, matrix products, body(): jnp.dot(residual, khatri, preferred_element_type=jnp.float32)  14.3 us
    all_gather x2, blocking collectives, body(): lax.all_gather(hour_factor.astype(jnp.bfloat16), 'camp', axis=0, tiled=True)  11.6 us
  transfers between devices with their start and end apart: 6, of which 2 were waited for; matrix products, arithmetic and copies ran while one was open for 4% of the time, Pallas kernels for 0%

commit v1 on v0

v1 whole, which is shorter than its diff:
```python
import math

import jax
import jax.numpy as jnp
from jax import lax
from jax.experimental import pallas as pl
from jax.experimental.pallas import tpu as pltpu
from jax.sharding import PartitionSpec as P

learn_rate = 0.1
beta_first = 0.9
beta_second = 0.999
adam_eps = 1e-08

F32 = jnp.float32
BF16 = jnp.bfloat16


def adam_update(factor, moment, second, gradient, grad_scale):
    scaled = gradient * grad_scale
    moment = beta_first * moment + (1.0 - beta_first) * scaled
    second = beta_second * second + (1.0 - beta_second) * scaled * scaled
    factor = factor - learn_rate * moment / (jnp.sqrt(second) + adam_eps)
    return (factor, moment, second)


def grads_kernel(prop_ref, obs_ref, bucket_ref, camp_ref, hour_ref, delay_ref, ga_ref, gb_ref, gc_ref, gb_sum, gc_sum):
    step = pl.program_id(0)
    rows, cols, delays = obs_ref.shape
    rank = hour_ref.shape[1]
    levels = prop_ref.shape[0]
    flat = rows * cols

    @pl.when(step == 0)
    def _():
        gb_sum[...] = jnp.zeros_like(gb_sum)
        gc_sum[...] = jnp.zeros_like(gc_sum)

    lane = lax.broadcasted_iota(jnp.int32, (8, delays), 1)
    chance = jnp.ones((8, delays), F32)
    for level in range(levels):
        chance = jnp.where(lane == level + 1, prop_ref[level], chance)
    table = jnp.where(lane == 0, 0.0, 1.0 / chance)
    table = jnp.broadcast_to(table[:1], (flat, delays))
    weight = jnp.take_along_axis(table, bucket_ref[...].reshape(flat, delays), axis=1)

    camp = camp_ref[...]
    hour = hour_ref[...]
    delay = delay_ref[...]
    pair = (camp[:, None, :] * hour[None, :, :]).reshape(flat, rank)
    model = lax.dot_general(pair, delay, (((1,), (1,)), ((), ())), preferred_element_type=F32)
    observed = obs_ref[...].reshape(flat, delays).astype(F32)
    residual = (weight * (model - observed)).astype(BF16)
    back = lax.dot_general(residual, delay, (((1,), (0,)), ((), ())), preferred_element_type=F32)
    back = back.reshape(rows, cols, rank)
    ga_ref[...] = jnp.sum(back * hour.astype(F32)[None, :, :], axis=1).astype(ga_ref.dtype)
    gb_sum[...] += jnp.sum(back * camp.astype(F32)[:, None, :], axis=0)
    gc_sum[...] += lax.dot_general(residual, pair, (((0,), (0,)), ((), ())), preferred_element_type=F32)

    @pl.when(step == pl.num_programs(0) - 1)
    def _():
        gb_ref[...] = gb_sum[...].astype(gb_ref.dtype)
        gc_ref[...] = gc_sum[...].astype(gc_ref.dtype)


def gradients(propensity, observed, bucket, camp_block, hour_block, delay_block):
    tile_rows, tile_cols, delay_count = observed.shape
    rank = camp_block.shape[1]
    rows = math.gcd(tile_rows, 16)

    def whole(shape):
        return pl.BlockSpec(shape, lambda i: (0,) * len(shape))

    tile = pl.BlockSpec((rows, tile_cols, delay_count), lambda i: (i, 0, 0))
    strip = pl.BlockSpec((rows, rank), lambda i: (i, 0))
    return pl.pallas_call(
        grads_kernel,
        grid=(tile_rows // rows,),
        in_specs=[
            pl.BlockSpec(memory_space=pltpu.SMEM),
            tile,
            tile,
            strip,
            whole((tile_cols, rank)),
            whole((delay_count, rank)),
        ],
        out_specs=[strip, whole((tile_cols, rank)), whole((delay_count, rank))],
        out_shape=[
            jax.ShapeDtypeStruct((tile_rows, rank), BF16),
            jax.ShapeDtypeStruct((tile_cols, rank), BF16),
            jax.ShapeDtypeStruct((delay_count, rank), BF16),
        ],
        scratch_shapes=[pltpu.VMEM((tile_cols, rank), F32), pltpu.VMEM((delay_count, rank), F32)],
        compiler_params=pltpu.CompilerParams(vmem_limit_bytes=48 * 1024 * 1024),
        cost_estimate=pl.CostEstimate(
            flops=6 * tile_rows * tile_cols * delay_count * rank,
            bytes_accessed=6 * tile_rows * tile_cols * delay_count,
            transcendentals=0,
        ),
        name="gradients",
    )(propensity, observed, bucket, camp_block, hour_block, delay_block)


def swap(block, axis, bit):
    size = lax.axis_size(axis)
    return lax.ppermute(block, axis, [(i, i ^ bit) for i in range(size)])


def bits_of(axis):
    size = lax.axis_size(axis)
    assert size & (size - 1) == 0
    return [1 << n for n in range(size.bit_length() - 1)]


def gather_blocks(block, axis):
    index = lax.axis_index(axis)
    for depth, bit in enumerate(reversed(bits_of(axis))):
        other = swap(block, axis, bit)
        high = (index & bit) != 0
        low_block = jnp.where(high, other, block)
        high_block = jnp.where(high, block, other)
        block = jnp.stack([low_block, high_block], axis=depth)
    count = lax.axis_size(axis)
    return block.reshape((count,) + block.shape[len(bits_of(axis)):])


def sum_step(block, axis, bit):
    total = block.astype(F32) + swap(block, axis, bit).astype(F32)
    return lax.optimization_barrier(total.astype(BF16))


def sum_all(camp_grad, hour_grad, delay_grad):
    cols = hour_grad.shape[0]
    rows = camp_grad.shape[0]
    joint = jnp.concatenate([hour_grad, delay_grad])
    for bit in bits_of("camp"):
        joint = sum_step(joint, "camp", bit)
    hour_sum, delay_part = joint[:cols], joint[cols:]
    joint = jnp.concatenate([camp_grad, delay_part])
    for bit in bits_of("hour"):
        joint = sum_step(joint, "hour", bit)
    return joint[:rows], hour_sum, joint[rows:]


def pack(factor, moment, second):
    high = factor.astype(BF16)
    return jnp.stack([high, moment.astype(BF16), second.astype(BF16)])


def own_rows(block, axis, count):
    return lax.dynamic_slice_in_dim(block, lax.axis_index(axis) * count, count, 0)


def body(
    observed,
    bucket,
    propensity,
    camp_factor,
    camp_moment,
    camp_second,
    hour_factor,
    hour_moment,
    hour_second,
    delay_factor,
    delay_moment,
    delay_second,
):
    tile_rows, tile_cols, delay_count = observed.shape
    camp_own, hour_own = camp_factor.shape[0], hour_factor.shape[0]
    campaigns = tile_rows * lax.axis_size("camp")
    total_hours = tile_cols * lax.axis_size("hour")
    rank = camp_factor.shape[1]
    camp_scale = 1.0 / math.sqrt(total_hours * delay_count)
    hour_scale = 1.0 / math.sqrt(campaigns * delay_count)
    delay_scale = 1.0 / math.sqrt(campaigns * total_hours)

    camp_all = gather_blocks(pack(camp_factor, camp_moment, camp_second), "hour")
    hour_all = gather_blocks(pack(hour_factor, hour_moment, hour_second), "camp")
    camp_all = [camp_all[:, n].reshape(tile_rows, rank) for n in range(3)]
    hour_all = [hour_all[:, n].reshape(tile_cols, rank) for n in range(3)]
    camp_block, hour_block, delay_block = camp_all[0], hour_all[0], delay_factor.astype(BF16)

    partial = gradients(propensity, observed, bucket, camp_block, hour_block, delay_block)
    camp_grad, hour_grad, delay_grad = (g.astype(F32) for g in sum_all(*partial))
    camp_block = adam_update(*(x.astype(F32) for x in camp_all), camp_grad, camp_scale)[0].astype(BF16)
    hour_block = adam_update(*(x.astype(F32) for x in hour_all), hour_grad, hour_scale)[0].astype(BF16)
    camp_state = adam_update(
        camp_factor, camp_moment, camp_second, own_rows(camp_grad, "hour", camp_own), camp_scale
    )
    hour_state = adam_update(
        hour_factor, hour_moment, hour_second, own_rows(hour_grad, "camp", hour_own), hour_scale
    )
    delay_state = adam_update(delay_factor, delay_moment, delay_second, delay_grad, delay_scale)
    delay_block = delay_state[0].astype(BF16)

    partial = gradients(propensity, observed, bucket, camp_block, hour_block, delay_block)
    camp_grad, hour_grad, delay_grad = (g.astype(F32) for g in sum_all(*partial))
    camp_new = adam_update(*camp_state, own_rows(camp_grad, "hour", camp_own), camp_scale)[0]
    hour_new = adam_update(*hour_state, own_rows(hour_grad, "camp", hour_own), hour_scale)[0]
    delay_new = adam_update(*delay_state, delay_grad, delay_scale)[0]
    return (camp_new, hour_new, delay_new)


def solution(mesh):
    in_specs = (
        P("camp", "hour", None),
        P("camp", "hour", None),
        P(),
        P(("camp", "hour"), None),
        P(("camp", "hour"), None),
        P(("camp", "hour"), None),
        P(("hour", "camp"), None),
        P(("hour", "camp"), None),
        P(("hour", "camp"), None),
        P(),
        P(),
        P(),
    )
    out_specs = (P(("camp", "hour"), None), P(("hour", "camp"), None), P())
    return jax.shard_map(body, mesh=mesh, in_specs=in_specs, out_specs=out_specs, check_vma=False)
```

time: 442 us -> 95.9 us (0.22)
  waiting for transfers between devices: 231 us -> 41.9 us
  blocking collectives: 73.5 us -> 0 us
  matrix products: 54.1 us -> 0 us
  other arithmetic: 49 us -> 6.98 us
  Pallas kernels: 0 us -> 23.2 us
  starting transfers between devices: 0.25 us -> 19.2 us
  between operations: 15.9 us -> 1.02 us
  local copies, waits for them, and re-layouts: 17.7 us -> 2.94 us
    psum x2 -> x0, waiting for transfers between devices: 229 us -> none  [body(): delay_grad = lax.psum(delay_grad, ('camp', 'hour'))]
    all_gather x4 -> x0, blocking collectives: 73.5 us -> none  [the longest x2 61.8 us: body(): lax.all_gather(camp_factor.astype(jnp.bfloat16), 'hour', axis=0, tiled=True)]
    dot_general x6 -> x0, matrix products: 54.1 us -> none  [the longest x2 22.5 us: local_terms(): lax.dot_general(camp_block, khatri, (((1,), (1,)), ((), ())), preferred_e...]
    ppermute x0 -> x15, waiting for transfers between devices: none -> 41.9 us  [swap(): return lax.ppermute(block, axis, [(i, i ^ bit) for i in range(size)])]
    pallas_call x0 -> x2, Pallas kernels: none -> 23.2 us  [gradients(): pl.pallas_call(grads_kernel, grid=(tile_rows // rows,), in_specs=[pl.Bloc...]
    ppermute x0 -> x15, starting transfers between devices: none -> 19.2 us  [swap(): return lax.ppermute(block, axis, [(i, i ^ bit) for i in range(size)])]
    reduce_sum x2 -> x0, other arithmetic: 16.6 us -> none  [local_terms(): jnp.sum(spread * hour_block.astype(jnp.float32)[:, None, :], axis=0)]
    add x1 -> x0, other arithmetic: 15.4 us -> none  [entry_weights(): weight + jnp.where(bucket == bucket_level + 1, inverse[bucket_level], jnp...]
  transfers between devices with their start and end apart: 6 -> 15, of which waited for: 2 -> 12; matrix products, arithmetic and copies ran while one was open for 4% -> 4% of each run, Pallas kernels for 0% -> 0%
where the time goes in v1:
time: 95.9 us; the launch traced here: 95.2 us
  waiting for transfers between devices  41.9 us (44%)
  Pallas kernels  23.2 us (24%)
  starting transfers between devices  19.2 us (20%)
  other arithmetic  6.98 us (7%)
  local copies, waits for them, and re-layouts  2.94 us (3%)
  between operations  1.02 us (1%)
    ppermute x15, waiting for transfers between devices, swap(): return lax.ppermute(block, axis, [(i, i ^ bit) for i in range(size)])  41.9 us
    pallas_call x2, Pallas kernels, gradients(): pl.pallas_call(grads_kernel, grid=(tile_rows // rows,), in_specs=[pl.Bloc...  23.2 us
    ppermute x15, starting transfers between devices, swap(): return lax.ppermute(block, axis, [(i, i ^ bit) for i in range(size)])  19.2 us
    another operation x6, other arithmetic, pack(): return jnp.stack([high, moment.astype(BF16), second.astype(BF16)])  3.02 us
    unnamed x24, local copies, waits for them, and re-layouts  2.9 us
    sub x3, other arithmetic, adam_update(): factor = factor - learn_rate * moment / (jnp.sqrt(second) + adam_eps)  2.18 us
  transfers between devices with their start and end apart: 15, of which 12 were waited for; matrix products, arithmetic and copies ran while one was open for 4% of the time, Pallas kernels for 0%

profile of v1, /device:TPU:0, one launch (start us, length us, event | category | flops | bytes accessed | tf_op | source)
XLA Modules:
  0.0 95.2 jit_solution(13873388204036502028)
XLA Ops:
  0.6 0.7 convert_bitcast_fusion.5
  1.4 0.7 convert_bitcast_fusion.3
  2.1 4.1 %collective-permute-start = (bf16[3,16,256]{2,1,0:T(8,128)(2,1)S(1)}, bf16[3,16,256]{2,1,0:T(8,128)(2,1)S(1)}, u32[]{:S(2)}, u32[]{:S(2)}) collective-permute-start(bf16[3,16,256]{2,1,0:T(8,128)(2,1)S(1)} %pad_maximum_fusion.8), channel_id=1, source_target_pairs={{0,4},{1,5},{2,6},{3,7},{4,0},{5,1},{6,2},{7,3},{8,12},{9,13},{10,... | collective-permute-start | bytes 73736 | tf_op jit(solution)/shard_map/ppermute | solution.py:106
  6.2 0.8 convert_bitcast_fusion.2
  7.0 0.8 convert_bitcast_fusion
  7.8 1.6 %collective-permute-start.3 = (bf16[3,32,256]{2,1,0:T(8,128)(2,1)S(1)}, bf16[3,32,256]{2,1,0:T(8,128)(2,1)S(1)}, u32[]{:S(2)}, u32[]{:S(2)}) collective-permute-start(bf16[3,32,256]{2,1,0:T(8,128)(2,1)S(1)} %pad_maximum_fusion.7), channel_id=1, source_target_pairs={{0,16},{8,24},{16,0},{24,8},{1,17},{9,25},{17,1},{25,9},{2,18},{10... | collective-permute-start | bytes 147464 | tf_op jit(solution)/shard_map/ppermute | solution.py:106
  9.3 0.9 convert_element_type.166.delay_ref
  10.3 1.6 %collective-permute-start.1 = (bf16[2,3,16,256]{3,2,1,0:T(8,128)(2,1)S(1)}, bf16[2,3,16,256]{3,2,1,0:T(8,128)(2,1)S(1)}, u32[]{:S(2)}, u32[]{:S(2)}) collective-permute-start(bf16[2,3,16,256]{3,2,1,0:T(8,128)(2,1)S(1)} %pad_maximum_fusion.6), channel_id=1, source_target_pairs={{0,2},{1,3},{2,0},{3,1},{4,6},{5,7},{6,4},{7,5},{8,10},{9,11},{10,... | collective-permute-start | bytes 147464 | tf_op jit(solution)/shard_map/ppermute | solution.py:106
  12.1 2.4 %collective-permute-done.1 = bf16[2,3,16,256]{3,2,1,0:T(8,128)(2,1)S(1)} collective-permute-done((bf16[2,3,16,256]{3,2,1,0:T(8,128)(2,1)S(1)}, bf16[2,3,16,256]{3,2,1,0:T(8,128)(2,1)S(1)}, u32[]{:S(2)}, u32[]{:S(2)}) %collective-permute-start.1) | collective-permute-done | bytes 49184 | tf_op jit(solution)/shard_map/ppermute | solution.py:106
  14.5 1.6 %collective-permute-start.2 = (bf16[2,2,3,16,256]{4,3,2,1,0:T(8,128)(2,1)S(1)}, bf16[2,2,3,16,256]{4,3,2,1,0:T(8,128)(2,1)S(1)}, u32[]{:S(2)}, u32[]{:S(2)}) collective-permute-start(bf16[2,2,3,16,256]{4,3,2,1,0:T(8,128)(2,1)S(1)} %pad_maximum_fusion.4), channel_id=1, source_target_pairs={{0,1},{1,0},{2,3},{3,2},{4,5},{5,4},{6,7},{7,6},{8,9},{9,8},{10,11... | collective-permute-start | bytes 294920 | tf_op jit(solution)/shard_map/ppermute | solution.py:106
  16.1 3.1 %collective-permute-done.2 = bf16[2,2,3,16,256]{4,3,2,1,0:T(8,128)(2,1)S(1)} collective-permute-done((bf16[2,2,3,16,256]{4,3,2,1,0:T(8,128)(2,1)S(1)}, bf16[2,2,3,16,256]{4,3,2,1,0:T(8,128)(2,1)S(1)}, u32[]{:S(2)}, u32[]{:S(2)}) %collective-permute-start.2) | collective-permute-done | bytes 98336 | tf_op jit(solution)/shard_map/ppermute | solution.py:106
  19.2 2.2 %copy-done = bf16[128,128,128]{2,1,0:T(8,128)(2,1)S(1)} copy-done((bf16[128,128,128]{2,1,0:T(8,128)(2,1)S(1)}, bf16[128,128,128]{2,1,0:T(8,128)(2,1)}, u32[]{:S(2)}) %copy-start) | copy-done | bytes 4194328
  21.4 0.7 copy-done.1
  22.1 11.6 %gradients.2 = (bf16[128,256]{1,0:T(8,128)(2,1)S(1)}, bf16[128,256]{1,0:T(8,128)(2,1)S(1)}, bf16[128,256]{1,0:T(8,128)(2,1)S(1)}) custom-call(f32[8]{0:T(128)S(1)} %copy-done.1, bf16[128,128,128]{2,1,0:T(8,128)(2,1)S(1)} %copy-done, s32[128,128,128]{2,1,0:T(8,128)} %bucket_ref.3, bf16[128,256]{1,0:T(8,128)(2,1)S(1)} %bitcast.85, ...), custom_call_target="tpu_custom_call" | custom-call | flops 3221225472 | bytes 12582912 | tf_op jit(solution)/shard_map/gradients/pallas_call | solution.py:76
  33.9 1.3 %collective-permute-done.5 = bf16[256,256]{1,0:T(8,128)(2,1)S(1)} collective-permute-done((bf16[256,256]{1,0:T(8,128)(2,1)S(1)}, bf16[256,256]{1,0:T(8,128)(2,1)S(1)}, u32[]{:S(2)}, u32[]{:S(2)}) %collective-permute-start.5) | collective-permute-done | bytes 131104 | tf_op jit(solution)/shard_map/ppermute | solution.py:106
  35.8 5.0 %collective-permute-done.6 = bf16[256,256]{1,0:T(8,128)(2,1)S(1)} collective-permute-done((bf16[256,256]{1,0:T(8,128)(2,1)S(1)}, bf16[256,256]{1,0:T(8,128)(2,1)S(1)}, u32[]{:S(2)}, u32[]{:S(2)}) %collective-permute-start.6) | collective-permute-done | bytes 131104 | tf_op jit(solution)/shard_map/ppermute | solution.py:106
  40.9 1.6 %collective-permute-start.7 = (bf16[256,256]{1,0:T(8,128)(2,1)S(1)}, bf16[256,256]{1,0:T(8,128)(2,1)S(1)}, u32[]{:S(2)}, u32[]{:S(2)}) collective-permute-start(bf16[256,256]{1,0:T(8,128)(2,1)S(1)} %pad_maximum_fusion.2), channel_id=1, source_target_pairs={{0,1},{1,0},{2,3},{3,2},{4,5},{5,4},{6,7},{7,6},{8,9},{9,8},{10,11... | collective-permute-start | bytes 393224 | tf_op jit(solution)/shard_map/ppermute | solution.py:106
  42.5 3.4 %collective-permute-done.7 = bf16[256,256]{1,0:T(8,128)(2,1)S(1)} collective-permute-done((bf16[256,256]{1,0:T(8,128)(2,1)S(1)}, bf16[256,256]{1,0:T(8,128)(2,1)S(1)}, u32[]{:S(2)}, u32[]{:S(2)}) %collective-permute-start.7) | collective-permute-done | bytes 131104 | tf_op jit(solution)/shard_map/ppermute | solution.py:106
  46.0 1.6 %collective-permute-start.8 = (bf16[256,256]{1,0:T(8,128)(2,1)S(1)}, bf16[256,256]{1,0:T(8,128)(2,1)S(1)}, u32[]{:S(2)}, u32[]{:S(2)}) collective-permute-start(bf16[256,256]{1,0:T(8,128)(2,1)S(1)} %add_convert_fusion.7), channel_id=1, source_target_pairs={{0,2},{1,3},{2,0},{3,1},{4,6},{5,7},{6,4},{7,5},{8,10},{9,11},{10,... | collective-permute-start | bytes 393224 | tf_op jit(solution)/shard_map/ppermute | solution.py:106
  47.7 3.6 %collective-permute-done.8 = bf16[256,256]{1,0:T(8,128)(2,1)S(1)} collective-permute-done((bf16[256,256]{1,0:T(8,128)(2,1)S(1)}, bf16[256,256]{1,0:T(8,128)(2,1)S(1)}, u32[]{:S(2)}, u32[]{:S(2)}) %collective-permute-start.8) | collective-permute-done | bytes 131104 | tf_op jit(solution)/shard_map/ppermute | solution.py:106
  51.9 5.3 %collective-permute-done.9 = bf16[256,256]{1,0:T(8,128)(2,1)S(1)} collective-permute-done((bf16[256,256]{1,0:T(8,128)(2,1)S(1)}, bf16[256,256]{1,0:T(8,128)(2,1)S(1)}, u32[]{:S(2)}, u32[]{:S(2)}) %collective-permute-start.9) | collective-permute-done | bytes 131104 | tf_op jit(solution)/shard_map/ppermute | solution.py:106
  57.6 11.6 %gradients.3 = (bf16[128,256]{1,0:T(8,128)(2,1)S(1)}, bf16[128,256]{1,0:T(8,128)(2,1)S(1)}, bf16[128,256]{1,0:T(8,128)(2,1)S(1)}) custom-call(f32[8]{0:T(128)S(1)} %copy-done.1, bf16[128,128,128]{2,1,0:T(8,128)(2,1)S(1)} %copy-done, s32[128,128,128]{2,1,0:T(8,128)} %bucket_ref.3, bf16[128,256]{1,0:T(8,128)(2,1)S(1)} %get-tuple-element.28.camp_ref, ...), custom_call_target="tpu_custom_call" | custom-call | flops 3221225472 | bytes 12582912 | tf_op jit(solution)/shard_map/gradients/pallas_call | solution.py:76
  69.3 1.3 %collective-permute-done.10 = bf16[256,256]{1,0:T(8,128)(2,1)S(1)} collective-permute-done((bf16[256,256]{1,0:T(8,128)(2,1)S(1)}, bf16[256,256]{1,0:T(8,128)(2,1)S(1)}, u32[]{:S(2)}, u32[]{:S(2)}) %collective-permute-start.10) | collective-permute-done | bytes 131104 | tf_op jit(solution)/shard_map/ppermute | solution.py:106
  70.7 1.7 %collective-permute-start.11 = (bf16[256,256]{1,0:T(8,128)(2,1)S(1)}, bf16[256,256]{1,0:T(8,128)(2,1)S(1)}, u32[]{:S(2)}, u32[]{:S(2)}) collective-permute-start(bf16[256,256]{1,0:T(8,128)(2,1)S(1)} %add_convert_fusion.4), channel_id=1, source_target_pairs={{0,16},{8,24},{16,0},{24,8},{1,17},{9,25},{17,1},{25,9},{2,18},{10... | collective-permute-start | bytes 393224 | tf_op jit(solution)/shard_map/ppermute | solution.py:106
  72.4 3.9 %collective-permute-done.11 = bf16[256,256]{1,0:T(8,128)(2,1)S(1)} collective-permute-done((bf16[256,256]{1,0:T(8,128)(2,1)S(1)}, bf16[256,256]{1,0:T(8,128)(2,1)S(1)}, u32[]{:S(2)}, u32[]{:S(2)}) %collective-permute-start.11) | collective-permute-done | bytes 131104 | tf_op jit(solution)/shard_map/ppermute | solution.py:106
  76.4 1.6 %collective-permute-start.12 = (bf16[256,256]{1,0:T(8,128)(2,1)S(1)}, bf16[256,256]{1,0:T(8,128)(2,1)S(1)}, u32[]{:S(2)}, u32[]{:S(2)}) collective-permute-start(bf16[256,256]{1,0:T(8,128)(2,1)S(1)} %pad_maximum_fusion.3), channel_id=1, source_target_pairs={{0,1},{1,0},{2,3},{3,2},{4,5},{5,4},{6,7},{7,6},{8,9},{9,8},{10,11... | collective-permute-start | bytes 393224 | tf_op jit(solution)/shard_map/ppermute | solution.py:106
  77.9 3.5 %collective-permute-done.12 = bf16[256,256]{1,0:T(8,128)(2,1)S(1)} collective-permute-done((bf16[256,256]{1,0:T(8,128)(2,1)S(1)}, bf16[256,256]{1,0:T(8,128)(2,1)S(1)}, u32[]{:S(2)}, u32[]{:S(2)}) %collective-permute-start.12) | collective-permute-done | bytes 131104 | tf_op jit(solution)/shard_map/ppermute | solution.py:106
  81.4 2.5 %collective-permute-start.13 = (bf16[256,256]{1,0:T(8,128)(2,1)S(1)}, bf16[256,256]{1,0:T(8,128)(2,1)S(1)}, u32[]{:S(2)}, u32[]{:S(2)}) collective-permute-start(bf16[256,256]{1,0:T(8,128)(2,1)S(1)} %add_convert_fusion.2), channel_id=1, source_target_pairs={{0,2},{1,3},{2,0},{3,1},{4,6},{5,7},{6,4},{7,5},{8,10},{9,11},{10,... | collective-permute-start | bytes 393224 | tf_op jit(solution)/shard_map/ppermute | solution.py:106
  84.0 3.7 %collective-permute-done.13 = bf16[256,256]{1,0:T(8,128)(2,1)S(1)} collective-permute-done((bf16[256,256]{1,0:T(8,128)(2,1)S(1)}, bf16[256,256]{1,0:T(8,128)(2,1)S(1)}, u32[]{:S(2)}, u32[]{:S(2)}) %collective-permute-start.13) | collective-permute-done | bytes 131104 | tf_op jit(solution)/shard_map/ppermute | solution.py:106
  87.8 0.7 fusion.28
  88.5 5.1 %collective-permute-done.14 = bf16[256,256]{1,0:T(8,128)(2,1)S(1)} collective-permute-done((bf16[256,256]{1,0:T(8,128)(2,1)S(1)}, bf16[256,256]{1,0:T(8,128)(2,1)S(1)}, u32[]{:S(2)}, u32[]{:S(2)}) %collective-permute-start.14) | collective-permute-done | bytes 131104 | tf_op jit(solution)/shard_map/ppermute | solution.py:106
  93.7 0.8 fusion.6
  (68 shorter events, 3.0 us)
Async XLA Ops:
  2.1 8.2 %collective-permute-start = (bf16[3,16,256]{2,1,0:T(8,128)(2,1)S(1)}, bf16[3,16,256]{2,1,0:T(8,128)(2,1)S(1)}, u32[]{:S(2)}, u32[]{:S(2)}) collective-permute-start(bf16[3,16,256]{2,1,0:T(8,128)(2,1)S(1)} %pad_maximum_fusion.8), channel_id=1, source_target_pairs={{0,4},{1,5},{2,6},{3,7},{4,0},{5,1},{6,2},{7,3},{8,12},{9,13},{10,... | collective-permute-start | bytes 73736 | tf_op jit(solution)/shard_map/ppermute | solution.py:106
  7.8 4.2 %collective-permute-start.3 = (bf16[3,32,256]{2,1,0:T(8,128)(2,1)S(1)}, bf16[3,32,256]{2,1,0:T(8,128)(2,1)S(1)}, u32[]{:S(2)}, u32[]{:S(2)}) collective-permute-start(bf16[3,32,256]{2,1,0:T(8,128)(2,1)S(1)} %pad_maximum_fusion.7), channel_id=1, source_target_pairs={{0,16},{8,24},{16,0},{24,8},{1,17},{9,25},{17,1},{25,9},{2,18},{10... | collective-permute-start | bytes 147464 | tf_op jit(solution)/shard_map/ppermute | solution.py:106
  10.3 4.2 %collective-permute-start.1 = (bf16[2,3,16,256]{3,2,1,0:T(8,128)(2,1)S(1)}, bf16[2,3,16,256]{3,2,1,0:T(8,128)(2,1)S(1)}, u32[]{:S(2)}, u32[]{:S(2)}) collective-permute-start(bf16[2,3,16,256]{3,2,1,0:T(8,128)(2,1)S(1)} %pad_maximum_fusion.6), channel_id=1, source_target_pairs={{0,2},{1,3},{2,0},{3,1},{4,6},{5,7},{6,4},{7,5},{8,10},{9,11},{10,... | collective-permute-start | bytes 147464 | tf_op jit(solution)/shard_map/ppermute | solution.py:106
  12.0 4.1 %collective-permute-start.4 = (bf16[2,3,32,256]{3,2,1,0:T(8,128)(2,1)S(1)}, bf16[2,3,32,256]{3,2,1,0:T(8,128)(2,1)S(1)}, u32[]{:S(2)}, u32[]{:S(2)}) collective-permute-start(bf16[2,3,32,256]{3,2,1,0:T(8,128)(2,1)S(1)} %pad_maximum_fusion.5), channel_id=1, source_target_pairs={{0,8},{8,0},{16,24},{24,16},{1,9},{9,1},{17,25},{25,17},{2,10},{10... | collective-permute-start | bytes 294920 | tf_op jit(solution)/shard_map/ppermute | solution.py:106
  14.5 4.7 %collective-permute-start.2 = (bf16[2,2,3,16,256]{4,3,2,1,0:T(8,128)(2,1)S(1)}, bf16[2,2,3,16,256]{4,3,2,1,0:T(8,128)(2,1)S(1)}, u32[]{:S(2)}, u32[]{:S(2)}) collective-permute-start(bf16[2,2,3,16,256]{4,3,2,1,0:T(8,128)(2,1)S(1)} %pad_maximum_fusion.4), channel_id=1, source_target_pairs={{0,1},{1,0},{2,3},{3,2},{4,5},{5,4},{6,7},{7,6},{8,9},{9,8},{10,11... | collective-permute-start | bytes 294920 | tf_op jit(solution)/shard_map/ppermute | solution.py:106
  19.2 2.2 %copy-start = (bf16[128,128,128]{2,1,0:T(8,128)(2,1)S(1)}, bf16[128,128,128]{2,1,0:T(8,128)(2,1)}, u32[]{:S(2)}) copy-start(bf16[128,128,128]{2,1,0:T(8,128)(2,1)} %obs_ref.3) | copy-start | bytes 12582916
  21.4 0.7 copy-start.1
  22.1 35.2 %copy-start.2 = (f32[128,256]{1,0:T(8,128)S(1)}, f32[128,256]{1,0:T(8,128)}, u32[]{:S(2)}) copy-start(f32[128,256]{1,0:T(8,128)} %param.21) | copy-start | bytes 393220
  22.1 35.2 %copy-start.3 = (f32[128,256]{1,0:T(8,128)S(1)}, f32[128,256]{1,0:T(8,128)}, u32[]{:S(2)}) copy-start(f32[128,256]{1,0:T(8,128)} %param.23) | copy-start | bytes 393220
  22.1 35.2 %copy-start.4 = (f32[128,256]{1,0:T(8,128)S(1)}, f32[128,256]{1,0:T(8,128)}, u32[]{:S(2)}) copy-start(f32[128,256]{1,0:T(8,128)} %param.22) | copy-start | bytes 393220
  33.8 1.4 %collective-permute-start.5 = (bf16[256,256]{1,0:T(8,128)(2,1)S(1)}, bf16[256,256]{1,0:T(8,128)(2,1)S(1)}, u32[]{:S(2)}, u32[]{:S(2)}) collective-permute-start(bf16[256,256]{1,0:T(8,128)(2,1)S(1)} %constant_dynamic-update-slice_fusion), channel_id=1, source_target_pairs={{0,8},{8,0},{16,24},{24,16},{1,9},{9,1},{17,25},{25,17},{2,10},{10... | collective-permute-start | bytes 393224 | tf_op jit(solution)/shard_map/ppermute | solution.py:106
  35.2 5.6 %collective-permute-start.6 = (bf16[256,256]{1,0:T(8,128)(2,1)S(1)}, bf16[256,256]{1,0:T(8,128)(2,1)S(1)}, u32[]{:S(2)}, u32[]{:S(2)}) collective-permute-start(bf16[256,256]{1,0:T(8,128)(2,1)S(1)} %add_convert_fusion.9), channel_id=1, source_target_pairs={{0,16},{8,24},{16,0},{24,8},{1,17},{9,25},{17,1},{25,9},{2,18},{10... | collective-permute-start | bytes 393224 | tf_op jit(solution)/shard_map/ppermute | solution.py:106
  40.9 5.0 %collective-permute-start.7 = (bf16[256,256]{1,0:T(8,128)(2,1)S(1)}, bf16[256,256]{1,0:T(8,128)(2,1)S(1)}, u32[]{:S(2)}, u32[]{:S(2)}) collective-permute-start(bf16[256,256]{1,0:T(8,128)(2,1)S(1)} %pad_maximum_fusion.2), channel_id=1, source_target_pairs={{0,1},{1,0},{2,3},{3,2},{4,5},{5,4},{6,7},{7,6},{8,9},{9,8},{10,11... | collective-permute-start | bytes 393224 | tf_op jit(solution)/shard_map/ppermute | solution.py:106
  46.0 5.3 %collective-permute-start.8 = (bf16[256,256]{1,0:T(8,128)(2,1)S(1)}, bf16[256,256]{1,0:T(8,128)(2,1)S(1)}, u32[]{:S(2)}, u32[]{:S(2)}) collective-permute-start(bf16[256,256]{1,0:T(8,128)(2,1)S(1)} %add_convert_fusion.7), channel_id=1, source_target_pairs={{0,2},{1,3},{2,0},{3,1},{4,6},{5,7},{6,4},{7,5},{8,10},{9,11},{10,... | collective-permute-start | bytes 393224 | tf_op jit(solution)/shard_map/ppermute | solution.py:106
  51.3 5.9 %collective-permute-start.9 = (bf16[256,256]{1,0:T(8,128)(2,1)S(1)}, bf16[256,256]{1,0:T(8,128)(2,1)S(1)}, u32[]{:S(2)}, u32[]{:S(2)}) collective-permute-start(bf16[256,256]{1,0:T(8,128)(2,1)S(1)} %add_convert_fusion.6), channel_id=1, source_target_pairs={{0,4},{1,5},{2,6},{3,7},{4,0},{5,1},{6,2},{7,3},{8,12},{9,13},{10,... | collective-permute-start | bytes 393224 | tf_op jit(solution)/shard_map/ppermute | solution.py:106
  51.9 35.9 %copy-start.5 = (f32[32,256]{1,0:T(8,128)S(1)}, f32[32,256]{1,0:T(8,128)}, u32[]{:S(2)}) copy-start(f32[32,256]{1,0:T(8,128)} %param.20) | copy-start | bytes 98308
  51.9 35.9 %copy-start.6 = (f32[32,256]{1,0:T(8,128)S(1)}, f32[32,256]{1,0:T(8,128)}, u32[]{:S(2)}) copy-start(f32[32,256]{1,0:T(8,128)} %param.19) | copy-start | bytes 98308
  51.9 35.9 %copy-start.7 = (f32[32,256]{1,0:T(8,128)S(1)}, f32[32,256]{1,0:T(8,128)}, u32[]{:S(2)}) copy-start(f32[32,256]{1,0:T(8,128)} %param.18) | copy-start | bytes 98308
  57.5 37.0 %copy-start.8 = (f32[16,256]{1,0:T(8,128)S(1)}, f32[16,256]{1,0:T(8,128)}, u32[]{:S(2)}) copy-start(f32[16,256]{1,0:T(8,128)} %param.17) | copy-start | bytes 49156
  57.5 37.0 %copy-start.9 = (f32[16,256]{1,0:T(8,128)S(1)}, f32[16,256]{1,0:T(8,128)}, u32[]{:S(2)}) copy-start(f32[16,256]{1,0:T(8,128)} %param.16) | copy-start | bytes 49156
  57.6 37.0 %copy-start.10 = (f32[16,256]{1,0:T(8,128)S(1)}, f32[16,256]{1,0:T(8,128)}, u32[]{:S(2)}) copy-start(f32[16,256]{1,0:T(8,128)} %param.15) | copy-start | bytes 49156
  69.2 1.4 %collective-permute-start.10 = (bf16[256,256]{1,0:T(8,128)(2,1)S(1)}, bf16[256,256]{1,0:T(8,128)(2,1)S(1)}, u32[]{:S(2)}, u32[]{:S(2)}) collective-permute-start(bf16[256,256]{1,0:T(8,128)(2,1)S(1)} %constant_dynamic-update-slice_fusion.2), channel_id=1, source_target_pairs={{0,8},{8,0},{16,24},{24,16},{1,9},{9,1},{17,25},{25,17},{2,10},{10... | collective-permute-start | bytes 393224 | tf_op jit(solution)/shard_map/ppermute | solution.py:106
  70.7 5.6 %collective-permute-start.11 = (bf16[256,256]{1,0:T(8,128)(2,1)S(1)}, bf16[256,256]{1,0:T(8,128)(2,1)S(1)}, u32[]{:S(2)}, u32[]{:S(2)}) collective-permute-start(bf16[256,256]{1,0:T(8,128)(2,1)S(1)} %add_convert_fusion.4), channel_id=1, source_target_pairs={{0,16},{8,24},{16,0},{24,8},{1,17},{9,25},{17,1},{25,9},{2,18},{10... | collective-permute-start | bytes 393224 | tf_op jit(solution)/shard_map/ppermute | solution.py:106
  76.4 5.0 %collective-permute-start.12 = (bf16[256,256]{1,0:T(8,128)(2,1)S(1)}, bf16[256,256]{1,0:T(8,128)(2,1)S(1)}, u32[]{:S(2)}, u32[]{:S(2)}) collective-permute-start(bf16[256,256]{1,0:T(8,128)(2,1)S(1)} %pad_maximum_fusion.3), channel_id=1, source_target_pairs={{0,1},{1,0},{2,3},{3,2},{4,5},{5,4},{6,7},{7,6},{8,9},{9,8},{10,11... | collective-permute-start | bytes 393224 | tf_op jit(solution)/shard_map/ppermute | solution.py:106
  81.4 6.3 %collective-permute-start.13 = (bf16[256,256]{1,0:T(8,128)(2,1)S(1)}, bf16[256,256]{1,0:T(8,128)(2,1)S(1)}, u32[]{:S(2)}, u32[]{:S(2)}) collective-permute-start(bf16[256,256]{1,0:T(8,128)(2,1)S(1)} %add_convert_fusion.2), channel_id=1, source_target_pairs={{0,2},{1,3},{2,0},{3,1},{4,6},{5,7},{6,4},{7,5},{8,10},{9,11},{10,... | collective-permute-start | bytes 393224 | tf_op jit(solution)/shard_map/ppermute | solution.py:106
  87.7 5.9 %collective-permute-start.14 = (bf16[256,256]{1,0:T(8,128)(2,1)S(1)}, bf16[256,256]{1,0:T(8,128)(2,1)S(1)}, u32[]{:S(2)}, u32[]{:S(2)}) collective-permute-start(bf16[256,256]{1,0:T(8,128)(2,1)S(1)} %add_convert_fusion.1), channel_id=1, source_target_pairs={{0,4},{1,5},{2,6},{3,7},{4,0},{5,1},{6,2},{7,3},{8,12},{9,13},{10,... | collective-permute-start | bytes 393224 | tf_op jit(solution)/shard_map/ppermute | solution.py:106

commit v2 on v1

v2 whole, which is shorter than its diff:
```python
import math

import jax
import jax.numpy as jnp
from jax import lax
from jax.experimental import pallas as pl
from jax.experimental.pallas import tpu as pltpu
from jax.sharding import PartitionSpec as P

learn_rate = 0.1
beta_first = 0.9
beta_second = 0.999
adam_eps = 1e-08

F32 = jnp.float32
BF16 = jnp.bfloat16


def adam_update(factor, moment, second, gradient, grad_scale):
    scaled = gradient * grad_scale
    moment = beta_first * moment + (1.0 - beta_first) * scaled
    second = beta_second * second + (1.0 - beta_second) * scaled * scaled
    factor = factor - learn_rate * moment / (jnp.sqrt(second) + adam_eps)
    return (factor, moment, second)


def grads_kernel(
    prop_ref, obs_hbm, bucket_hbm, camp_ref, hour_ref, delay_ref,
    ga_ref, gb_ref, gc_ref, gb_sum, gc_sum, obs_ref, bucket_ref, sems,
):
    total, cols, delays = obs_ref.shape
    rank = hour_ref.shape[1]
    parts = sems.shape[1]
    rows = total // parts
    sub = math.gcd(rows, 8)
    flat = sub * cols

    def fetches(part):
        at = pl.ds(part * rows, rows)
        return (
            pltpu.make_async_copy(obs_hbm.at[at], obs_ref.at[at], sems.at[0, part]),
            pltpu.make_async_copy(bucket_hbm.at[at], bucket_ref.at[at], sems.at[1, part]),
        )

    for part in range(parts):
        for fetch in fetches(part):
            fetch.start()

    gb_sum[...] = jnp.zeros_like(gb_sum)
    gc_sum[...] = jnp.zeros_like(gc_sum)
    lane = lax.broadcasted_iota(jnp.int32, (8, delays), 1)
    chance = jnp.ones((8, delays), F32)
    for level in range(prop_ref.shape[0]):
        chance = jnp.where(lane == level + 1, prop_ref[level], chance)
    table = jnp.where(lane == 0, 0.0, 1.0 / chance)
    table = jnp.broadcast_to(table[:1], (flat, delays))

    hour16 = hour_ref[...]
    hour = hour16.astype(F32)
    delay = delay_ref[...]

    for part in range(parts):
        for fetch in fetches(part):
            fetch.wait()
        gb_part, gc_part = gb_sum[...], gc_sum[...]
        for start in range(part * rows, (part + 1) * rows, sub):
            camp = camp_ref[start:start + sub]
            pair = (camp[:, None, :] * hour16[None, :, :]).reshape(flat, rank)
            model = lax.dot_general(pair, delay, (((1,), (1,)), ((), ())), preferred_element_type=F32)
            bucket = bucket_ref[start:start + sub].reshape(flat, delays)
            weight = jnp.take_along_axis(table, bucket, axis=1)
            observed = obs_ref[start:start + sub].reshape(flat, delays).astype(F32)
            residual = (weight * (model - observed)).astype(BF16)
            back = jnp.dot(residual, delay, preferred_element_type=F32).reshape(sub, cols, rank)
            ga_ref[start:start + sub] = jnp.sum(back * hour[None, :, :], axis=1)
            gb_part += jnp.sum(back * camp.astype(F32)[:, None, :], axis=0)
            gc_part += lax.dot_general(residual, pair, (((0,), (0,)), ((), ())), preferred_element_type=F32)
        gb_sum[...] = gb_part
        gc_sum[...] = gc_part
    gb_ref[...] = gb_sum[...].astype(gb_ref.dtype)
    gc_ref[...] = gc_sum[...].astype(gc_ref.dtype)


def gradients(propensity, observed, bucket, camp_block, hour_block, delay_block):
    tile_rows, tile_cols, delay_count = observed.shape
    rank = camp_block.shape[1]
    parts = tile_rows // math.gcd(tile_rows, 16)
    vmem = pl.BlockSpec(memory_space=pltpu.VMEM)
    hbm = pl.BlockSpec(memory_space=pltpu.HBM)
    observed, bucket = (pltpu.with_memory_space_constraint(x, pltpu.HBM) for x in (observed, bucket))
    return pl.pallas_call(
        grads_kernel,
        in_specs=[pl.BlockSpec(memory_space=pltpu.SMEM), hbm, hbm, vmem, vmem, vmem],
        out_specs=[vmem, vmem, vmem],
        out_shape=[
            jax.ShapeDtypeStruct((tile_rows, rank), F32),
            jax.ShapeDtypeStruct((tile_cols, rank), BF16),
            jax.ShapeDtypeStruct((delay_count, rank), BF16),
        ],
        scratch_shapes=[
            pltpu.VMEM((tile_cols, rank), F32),
            pltpu.VMEM((delay_count, rank), F32),
            pltpu.VMEM(observed.shape, observed.dtype),
            pltpu.VMEM(bucket.shape, bucket.dtype),
            pltpu.SemaphoreType.DMA((2, parts)),
        ],
        compiler_params=pltpu.CompilerParams(vmem_limit_bytes=40 * 1024 * 1024),
        cost_estimate=pl.CostEstimate(
            flops=6 * tile_rows * tile_cols * delay_count * rank,
            bytes_accessed=6 * tile_rows * tile_cols * delay_count,
            transcendentals=0,
        ),
        name="gradients",
    )(propensity, observed, bucket, camp_block, hour_block, delay_block)


def pack_kernel(*refs):
    camp, hour, delay, camp_out, hour_out, delay_out = refs[:3], refs[3:6], refs[6], *refs[7:]
    for n in range(3):
        camp_out[n] = camp[n][...].astype(BF16)
        hour_out[n] = hour[n][...].astype(BF16)
    delay_out[...] = delay[...].astype(BF16)


def pack(camp, hour, delay):
    vmem = pl.BlockSpec(memory_space=pltpu.VMEM)
    return pl.pallas_call(
        pack_kernel,
        in_specs=[vmem] * 7,
        out_specs=[vmem] * 3,
        out_shape=[
            jax.ShapeDtypeStruct((3,) + camp[0].shape, BF16),
            jax.ShapeDtypeStruct((3,) + hour[0].shape, BF16),
            jax.ShapeDtypeStruct(delay.shape, BF16),
        ],
        name="pack",
    )(*camp, *hour, delay)


def swap(block, axis, bit):
    size = lax.axis_size(axis)
    return lax.ppermute(block, axis, [(i, i ^ bit) for i in range(size)])


def bits_of(axis):
    size = lax.axis_size(axis)
    assert size & (size - 1) == 0
    return [1 << n for n in range(size.bit_length() - 1)]


def gather_blocks(block, axis):
    index = lax.axis_index(axis)
    for depth, bit in enumerate(reversed(bits_of(axis))):
        other = swap(block, axis, bit)
        high = (index & bit) != 0
        low_block = jnp.where(high, other, block)
        high_block = jnp.where(high, block, other)
        block = jnp.stack([low_block, high_block], axis=depth)
    count = lax.axis_size(axis)
    return block.reshape((count,) + block.shape[len(bits_of(axis)):])


def swap_both(block, camp_bit, hour_bit):
    hours = lax.axis_size("hour")
    size = lax.axis_size("camp") * hours
    return lax.ppermute(block, ("camp", "hour"), [(i, i ^ (camp_bit * hours + hour_bit)) for i in range(size)])


def add(*terms):
    terms = [t.astype(F32) for t in terms]
    while len(terms) > 1:
        terms = [terms[n] + terms[n + 1] for n in range(0, len(terms), 2)]
    return terms[0]


def rounded(block):
    return lax.optimization_barrier(block.astype(BF16))


class Rows:
    def __init__(self, block, axis, whole):
        self.axis, self.whole, self.bits = axis, whole, bits_of(axis)[::-1]
        self.block = block
        if not whole:
            rows, rank = block.shape
            own = rows >> len(self.bits)
            self.block = block.reshape((2,) * len(self.bits) + (own, rank))

    def send(self, bit):
        if self.whole:
            return self.block
        at = self.bits.index(bit)
        low, high = (lax.index_in_dim(self.block, n, at, keepdims=False) for n in (0, 1))
        is_high = (lax.axis_index(self.axis) & bit) != 0
        self.block = jnp.where(is_high, high, low)
        self.bits.remove(bit)
        return jnp.where(is_high, low, high)

    def receive(self, other):
        self.block = rounded(add(self.block, other))


def exchange(gradient, bit, extra):
    sent = gradient.send(bit)
    rank = sent.shape[-1]
    joint = jnp.concatenate([sent.reshape(-1, rank), extra])
    joint = swap(joint, gradient.axis, bit)
    gradient.receive(joint[:-extra.shape[0]].reshape(sent.shape))
    return joint[-extra.shape[0]:]


def sum_all(camp_grad, hour_grad, delay_grad, whole):
    camp_bits, hour_bits = bits_of("camp"), bits_of("hour")
    camp_rows = Rows(camp_grad.astype(BF16), "hour", whole)
    hour_rows = Rows(hour_grad, "camp", whole)
    first = camp_bits.pop(0)
    half = delay_grad.shape[0] // 2
    is_high = (lax.axis_index("camp") & first) != 0
    low, high = delay_grad[:half], delay_grad[half:]
    kept = jnp.where(is_high, high, low)
    delay_part = rounded(add(kept, exchange(hour_rows, first, jnp.where(is_high, low, high))))
    while camp_bits and hour_bits:
        camp_bit, hour_bit = camp_bits.pop(0), hour_bits.pop(0)
        other_camp = exchange(hour_rows, camp_bit, delay_part)
        other_hour = exchange(camp_rows, hour_bit, delay_part)
        other_both = swap_both(delay_part, camp_bit, hour_bit)
        delay_part = rounded(add(delay_part, other_hour, other_camp, other_both))
    for rows, bits in ((hour_rows, camp_bits), (camp_rows, hour_bits)):
        for bit in bits:
            delay_part = rounded(add(delay_part, exchange(rows, bit, delay_part)))
    other = swap(delay_part, "camp", first)
    delay_sum = jnp.concatenate([jnp.where(is_high, other, delay_part), jnp.where(is_high, delay_part, other)])
    return camp_rows.block.astype(F32), hour_rows.block.astype(F32), delay_sum.astype(F32)


def own_rows(block, axis, count):
    return lax.dynamic_slice_in_dim(block, lax.axis_index(axis) * count, count, 0)


def body(
    observed,
    bucket,
    propensity,
    camp_factor,
    camp_moment,
    camp_second,
    hour_factor,
    hour_moment,
    hour_second,
    delay_factor,
    delay_moment,
    delay_second,
):
    tile_rows, tile_cols, delay_count = observed.shape
    camp_own, hour_own = camp_factor.shape[0], hour_factor.shape[0]
    campaigns = tile_rows * lax.axis_size("camp")
    total_hours = tile_cols * lax.axis_size("hour")
    rank = camp_factor.shape[1]
    camp_scale = 1.0 / math.sqrt(total_hours * delay_count)
    hour_scale = 1.0 / math.sqrt(campaigns * delay_count)
    delay_scale = 1.0 / math.sqrt(campaigns * total_hours)

    camp_state = (camp_factor, camp_moment, camp_second)
    hour_state = (hour_factor, hour_moment, hour_second)
    camp_packed, hour_packed, delay_block = pack(camp_state, hour_state, delay_factor)
    camp_all = gather_blocks(camp_packed, "hour")
    hour_all = gather_blocks(hour_packed, "camp")
    camp_all = [camp_all[:, n].reshape(tile_rows, rank) for n in range(3)]
    hour_all = [hour_all[:, n].reshape(tile_cols, rank) for n in range(3)]
    camp_block, hour_block = camp_all[0], hour_all[0]

    partial = gradients(propensity, observed, bucket, camp_block, hour_block, delay_block)
    camp_grad, hour_grad, delay_grad = sum_all(*partial, whole=True)
    camp_block = adam_update(*(x.astype(F32) for x in camp_all), camp_grad, camp_scale)[0].astype(BF16)
    hour_block = adam_update(*(x.astype(F32) for x in hour_all), hour_grad, hour_scale)[0].astype(BF16)
    camp_state = adam_update(*camp_state, own_rows(camp_grad, "hour", camp_own), camp_scale)
    hour_state = adam_update(*hour_state, own_rows(hour_grad, "camp", hour_own), hour_scale)
    delay_state = adam_update(delay_factor, delay_moment, delay_second, delay_grad, delay_scale)
    delay_block = delay_state[0].astype(BF16)

    partial = gradients(propensity, observed, bucket, camp_block, hour_block, delay_block)
    camp_grad, hour_grad, delay_grad = sum_all(*partial, whole=False)
    camp_new = adam_update(*camp_state, camp_grad, camp_scale)[0]
    hour_new = adam_update(*hour_state, hour_grad, hour_scale)[0]
    delay_new = adam_update(*delay_state, delay_grad, delay_scale)[0]
    return (camp_new, hour_new, delay_new)


def solution(mesh):
    in_specs = (
        P("camp", "hour", None),
        P("camp", "hour", None),
        P(),
        P(("camp", "hour"), None),
        P(("camp", "hour"), None),
        P(("camp", "hour"), None),
        P(("hour", "camp"), None),
        P(("hour", "camp"), None),
        P(("hour", "camp"), None),
        P(),
        P(),
        P(),
    )
    out_specs = (P(("camp", "hour"), None), P(("hour", "camp"), None), P())
    return jax.shard_map(body, mesh=mesh, in_specs=in_specs, out_specs=out_specs, check_vma=False)
```

time: 95.9 us -> 82.5 us (0.86)
  waiting for transfers between devices: 41.9 us -> 27 us
  starting transfers between devices: 19.2 us -> 24.7 us
  other arithmetic: 6.98 us -> 4.66 us
  local copies, waits for them, and re-layouts: 2.94 us -> 1.61 us
    ppermute x15 -> x17, waiting for transfers between devices: 41.9 us -> 25.8 us  [swap(): return lax.ppermute(block, axis, [(i, i ^ bit) for i in range(size)])]
    ppermute x0 -> x2, starting transfers between devices: none -> 4.5 us  [swap_both(): lax.ppermute(block, ('camp', 'hour'), [(i, i ^ camp_bit * hours + hour_bi...]
    another operation x6 -> x0, other arithmetic: 3.02 us -> none  [pack(): return jnp.stack([high, moment.astype(BF16), second.astype(BF16)])]
    another operation x10, other arithmetic: 0.15 us -> 1.68 us  [gather_blocks(): block = jnp.stack([low_block, high_block], axis=depth)]
    unnamed x24, local copies, waits for them, and re-layouts: 2.9 us -> 1.54 us
    ppermute x0 -> x2, waiting for transfers between devices: none -> 1.21 us  [swap_both(): lax.ppermute(block, ('camp', 'hour'), [(i, i ^ camp_bit * hours + hour_bi...]
    ppermute x15 -> x17, starting transfers between devices: 19.2 us -> 20.2 us  [swap(): return lax.ppermute(block, axis, [(i, i ^ bit) for i in range(size)])]
    pallas_call x2 -> x3, Pallas kernels: 23.2 us -> 23.1 us  [the longest x2 21.4 us: gradients(): pl.pallas_call(grads_kernel, in_specs=[pl.BlockSpec(memory_space=pltpu.SM...]
  transfers between devices with their start and end apart: 15 -> 19, of which waited for: 12 -> 15; matrix products, arithmetic and copies ran while one was open for 4% -> 4% of each run, Pallas kernels for 0% -> 0%
where the time goes in v2:
time: 82.5 us; the launch traced here: 82.2 us
  waiting for transfers between devices  27 us (33%)
  starting transfers between devices  24.7 us (30%)
  Pallas kernels  23.1 us (28%)
  other arithmetic  4.66 us (6%)
  local copies, waits for them, and re-layouts  1.61 us (2%)
  between operations  1.15 us (1%)
    ppermute x17, waiting for transfers between devices, swap(): return lax.ppermute(block, axis, [(i, i ^ bit) for i in range(size)])  25.8 us
    pallas_call x2, Pallas kernels, gradients(): pl.pallas_call(grads_kernel, in_specs=[pl.BlockSpec(memory_space=pltpu.SM...  21.4 us
    ppermute x17, starting transfers between devices, swap(): return lax.ppermute(block, axis, [(i, i ^ bit) for i in range(size)])  20.2 us
    ppermute x2, starting transfers between devices, swap_both(): lax.ppermute(block, ('camp', 'hour'), [(i, i ^ camp_bit * hours + hour_bi...  4.5 us
    sub x3, other arithmetic, adam_update(): factor = factor - learn_rate * moment / (jnp.sqrt(second) + adam_eps)  2.17 us
    pallas_call x1, Pallas kernels, pack(): pl.pallas_call(pack_kernel, in_specs=[vmem] * 7, out_specs=[vmem] * 3, ou...  1.68 us
    another operation x10, other arithmetic, gather_blocks(): block = jnp.stack([low_block, high_block], axis=depth)  1.68 us
  transfers between devices with their start and end apart: 19, of which 15 were waited for; matrix products, arithmetic and copies ran while one was open for 4% of the time, Pallas kernels for 0%

profile of v2, /device:TPU:0, one launch (start us, length us, event | category | flops | bytes accessed | tf_op | source)
XLA Modules:
  0.0 82.2 jit_solution(5758055729651339674)
XLA Ops:
  0.6 1.7 %pack.1 = (bf16[3,16,256]{2,1,0:T(8,128)(2,1)}, bf16[3,32,256]{2,1,0:T(8,128)(2,1)}, bf16[128,256]{1,0:T(8,128)(2,1)}) custom-call(f32[16,256]{1,0:T(8,128)} %refs_0_.1, f32[16,256]{1,0:T(8,128)} %refs_1_.1, f32[16,256]{1,0:T(8,128)} %refs_2_.1, f32[32,256]{1,0:T(8,128)} %refs_3_.1, f32[32,256]{1,0:T(8,128)} %refs_4_.1, f32[32,256]{1,0:T(8,128)} %refs_5_.1, ...), custom_call_target="tpu_custom_call" | custom-call | tf_op jit(solution)/shard_map/pack/pallas_call | solution.py:127
  2.3 4.0 %collective-permute-start = (bf16[3,16,256]{2,1,0:T(8,128)(2,1)}, bf16[3,16,256]{2,1,0:T(8,128)(2,1)S(1)}, u32[]{:S(2)}, u32[]{:S(2)}) collective-permute-start(bf16[3,16,256]{2,1,0:T(8,128)(2,1)} %get-tuple-element.12), channel_id=1, source_target_pairs={{0,4},{1,5},{2,6},{3,7},{4,0},{5,1},{6,2},{7,3},{8,12},{9,13},{10,... | collective-permute-start | bytes 73736 | tf_op jit(solution)/shard_map/ppermute | solution.py:142
  6.3 1.5 %collective-permute-start.3 = (bf16[3,32,256]{2,1,0:T(8,128)(2,1)}, bf16[3,32,256]{2,1,0:T(8,128)(2,1)S(1)}, u32[]{:S(2)}, u32[]{:S(2)}) collective-permute-start(bf16[3,32,256]{2,1,0:T(8,128)(2,1)} %get-tuple-element.13), channel_id=1, source_target_pairs={{0,16},{8,24},{16,0},{24,8},{1,17},{9,25},{17,1},{25,9},{2,18},{10... | collective-permute-start | bytes 147464 | tf_op jit(solution)/shard_map/ppermute | solution.py:142
  8.4 0.7 select_bitcast_fusion.9
  9.1 2.0 %collective-permute-start.1 = (bf16[2,3,16,256]{3,2,1,0:T(8,128)(2,1)S(1)}, bf16[2,3,16,256]{3,2,1,0:T(8,128)(2,1)S(1)}, u32[]{:S(2)}, u32[]{:S(2)}) collective-permute-start(bf16[2,3,16,256]{3,2,1,0:T(8,128)(2,1)S(1)} %pad_maximum_fusion.12), channel_id=1, source_target_pairs={{0,2},{1,3},{2,0},{3,1},{4,6},{5,7},{6,4},{7,5},{8,10},{9,11},{10,... | collective-permute-start | bytes 147464 | tf_op jit(solution)/shard_map/ppermute | solution.py:142
  11.1 0.8 select_bitcast_fusion.5
  12.0 1.3 %collective-permute-done.1 = bf16[2,3,16,256]{3,2,1,0:T(8,128)(2,1)S(1)} collective-permute-done((bf16[2,3,16,256]{3,2,1,0:T(8,128)(2,1)S(1)}, bf16[2,3,16,256]{3,2,1,0:T(8,128)(2,1)S(1)}, u32[]{:S(2)}, u32[]{:S(2)}) %collective-permute-start.1) | collective-permute-done | bytes 49184 | tf_op jit(solution)/shard_map/ppermute | solution.py:142
  13.3 2.0 %collective-permute-start.2 = (bf16[2,2,3,16,256]{4,3,2,0,1:T(8,128)(2,1)S(1)}, bf16[2,2,3,16,256]{4,3,2,0,1:T(8,128)(2,1)S(1)}, u32[]{:S(2)}, u32[]{:S(2)}) collective-permute-start(bf16[2,2,3,16,256]{4,3,2,0,1:T(8,128)(2,1)S(1)} %pad_maximum_fusion.4), channel_id=1, source_target_pairs={{0,1},{1,0},{2,3},{3,2},{4,5},{5,4},{6,7},{7,6},{8,9},{9,8},{10,11... | collective-permute-start | bytes 294920 | tf_op jit(solution)/shard_map/ppermute | solution.py:142
  15.4 2.6 %collective-permute-done.2 = bf16[2,2,3,16,256]{4,3,2,0,1:T(8,128)(2,1)S(1)} collective-permute-done((bf16[2,2,3,16,256]{4,3,2,0,1:T(8,128)(2,1)S(1)}, bf16[2,2,3,16,256]{4,3,2,0,1:T(8,128)(2,1)S(1)}, u32[]{:S(2)}, u32[]{:S(2)}) %collective-permute-start.2) | collective-permute-done | bytes 98336 | tf_op jit(solution)/shard_map/ppermute | solution.py:142
  18.1 0.8 %copy-done = bf16[128,256]{1,0:T(8,128)(2,1)S(1)} copy-done((bf16[128,256]{1,0:T(8,128)(2,1)S(1)}, bf16[128,256]{1,0:T(8,128)(2,1)}, u32[]{:S(2)}) %copy-start) | copy-done | bytes 65560
  18.9 0.7 copy-done.1
  19.6 10.6 %gradients.2 = (f32[128,256]{1,0:T(8,128)S(1)}, bf16[128,256]{1,0:T(8,128)(2,1)S(1)}, bf16[128,256]{1,0:T(8,128)(2,1)S(1)}) custom-call(f32[8]{0:T(128)S(1)} %copy-done.1, bf16[128,128,128]{2,1,0:T(8,128)(2,1)} %obs_hbm.3, s32[128,128,128]{2,1,0:T(8,128)} %bucket_hbm.3, bf16[128,256]{1,0:T(8,128)(2,1)S(1)} %bitcast.109, bf16[128,256]{1,0:T(8,128)(2,1)S(1)} %bitcast.108, ...), custom_call_target="tpu_custom_call" | custom-call | flops 3221225472 | bytes 12582912 | tf_op jit(solution)/shard_map/gradients/pallas_call | solution.py:91
  30.4 1.3 %collective-permute-done.5 = bf16[192,256]{1,0:T(8,128)(2,1)S(1)} collective-permute-done((bf16[192,256]{1,0:T(8,128)(2,1)S(1)}, bf16[192,256]{1,0:T(8,128)(2,1)S(1)}, u32[]{:S(2)}, u32[]{:S(2)}) %collective-permute-start.5) | collective-permute-done | bytes 98336 | tf_op jit(solution)/shard_map/ppermute | solution.py:142
  31.7 3.0 %collective-permute-start.8 = (bf16[64,256]{1,0:T(8,128)(2,1)S(1)}, bf16[64,256]{1,0:T(8,128)(2,1)S(1)}, u32[]{:S(2)}, u32[]{:S(2)}) collective-permute-start(bf16[64,256]{1,0:T(8,128)(2,1)S(1)} %add_convert_fusion.12), channel_id=1, source_target_pairs={{0,17},{1,16},{2,19},{3,18},{4,21},{5,20},{6,23},{7,22},{8,25},{9,... | collective-permute-start | bytes 98312 | tf_op jit(solution)/shard_map/ppermute | solution.py:166
  35.3 1.2 %collective-permute-done.8 = bf16[64,256]{1,0:T(8,128)(2,1)S(1)} collective-permute-done((bf16[64,256]{1,0:T(8,128)(2,1)S(1)}, bf16[64,256]{1,0:T(8,128)(2,1)S(1)}, u32[]{:S(2)}, u32[]{:S(2)}) %collective-permute-start.8) | collective-permute-done | bytes 32800 | tf_op jit(solution)/shard_map/ppermute | solution.py:166
  36.5 2.8 %collective-permute-done.6 = bf16[192,256]{1,0:T(8,128)(2,1)S(1)} collective-permute-done((bf16[192,256]{1,0:T(8,128)(2,1)S(1)}, bf16[192,256]{1,0:T(8,128)(2,1)S(1)}, u32[]{:S(2)}, u32[]{:S(2)}) %collective-permute-start.6) | collective-permute-done | bytes 98336 | tf_op jit(solution)/shard_map/ppermute | solution.py:142
  39.9 1.5 %collective-permute-start.9 = (bf16[192,256]{1,0:T(8,128)(2,1)S(1)}, bf16[192,256]{1,0:T(8,128)(2,1)S(1)}, u32[]{:S(2)}, u32[]{:S(2)}) collective-permute-start(bf16[192,256]{1,0:T(8,128)(2,1)S(1)} %pad_maximum_fusion.7), channel_id=1, source_target_pairs={{0,2},{1,3},{2,0},{3,1},{4,6},{5,7},{6,4},{7,5},{8,10},{9,11},{10,... | collective-permute-start | bytes 294920 | tf_op jit(solution)/shard_map/ppermute | solution.py:142
  41.5 3.2 %collective-permute-done.9 = bf16[192,256]{1,0:T(8,128)(2,1)S(1)} collective-permute-done((bf16[192,256]{1,0:T(8,128)(2,1)S(1)}, bf16[192,256]{1,0:T(8,128)(2,1)S(1)}, u32[]{:S(2)}, u32[]{:S(2)}) %collective-permute-start.9) | collective-permute-done | bytes 98336 | tf_op jit(solution)/shard_map/ppermute | solution.py:142
  44.7 2.5 %collective-permute-start.10 = (bf16[192,256]{1,0:T(8,128)(2,1)S(1)}, bf16[192,256]{1,0:T(8,128)(2,1)S(1)}, u32[]{:S(2)}, u32[]{:S(2)}) collective-permute-start(bf16[192,256]{1,0:T(8,128)(2,1)S(1)} %pad_maximum_fusion.8), channel_id=1, source_target_pairs={{0,4},{1,5},{2,6},{3,7},{4,0},{5,1},{6,2},{7,3},{8,12},{9,13},{10,... | collective-permute-start | bytes 294920 | tf_op jit(solution)/shard_map/ppermute | solution.py:142
  47.2 4.1 %collective-permute-done.10 = bf16[192,256]{1,0:T(8,128)(2,1)S(1)} collective-permute-done((bf16[192,256]{1,0:T(8,128)(2,1)S(1)}, bf16[192,256]{1,0:T(8,128)(2,1)S(1)}, u32[]{:S(2)}, u32[]{:S(2)}) %collective-permute-start.10) | collective-permute-done | bytes 98336 | tf_op jit(solution)/shard_map/ppermute | solution.py:142
  51.7 0.9 %collective-permute-done.11 = bf16[64,256]{1,0:T(8,128)(2,1)S(1)} collective-permute-done((bf16[64,256]{1,0:T(8,128)(2,1)S(1)}, bf16[64,256]{1,0:T(8,128)(2,1)S(1)}, u32[]{:S(2)}, u32[]{:S(2)}) %collective-permute-start.11) | collective-permute-done | bytes 32800 | tf_op jit(solution)/shard_map/ppermute | solution.py:142
  52.8 10.8 %gradients.3 = (f32[128,256]{1,0:T(8,128)S(1)}, bf16[128,256]{1,0:T(8,128)(2,1)S(1)}, bf16[128,256]{1,0:T(8,128)(2,1)S(1)}) custom-call(f32[8]{0:T(128)S(1)} %copy-done.2, bf16[128,128,128]{2,1,0:T(8,128)(2,1)} %obs_hbm.3, s32[128,128,128]{2,1,0:T(8,128)} %bucket_hbm.3, bf16[128,256]{1,0:T(8,128)(2,1)S(1)} %get-tuple-element.43.camp_ref, ...), custom_call_target="tpu_custom_call" | custom-call | flops 3221225472 | bytes 12582912 | tf_op jit(solution)/shard_map/gradients/pallas_call | solution.py:91
  63.9 1.1 %collective-permute-done.12 = bf16[128,256]{1,0:T(8,128)(2,1)S(1)} collective-permute-done((bf16[128,256]{1,0:T(8,128)(2,1)S(1)}, bf16[128,256]{1,0:T(8,128)(2,1)S(1)}, u32[]{:S(2)}, u32[]{:S(2)}) %collective-permute-start.12) | collective-permute-done | bytes 65568 | tf_op jit(solution)/shard_map/ppermute | solution.py:142
  65.0 1.5 %collective-permute-start.15 = (bf16[64,256]{1,0:T(8,128)(2,1)S(1)}, bf16[64,256]{1,0:T(8,128)(2,1)S(1)}, u32[]{:S(2)}, u32[]{:S(2)}) collective-permute-start(bf16[64,256]{1,0:T(8,128)(2,1)S(1)} %add_convert_fusion.8), channel_id=1, source_target_pairs={{0,17},{1,16},{2,19},{3,18},{4,21},{5,20},{6,23},{7,22},{8,25},{9,... | collective-permute-start | bytes 98312 | tf_op jit(solution)/shard_map/ppermute | solution.py:166
  66.7 2.0 %collective-permute-start.14 = (bf16[96,256]{1,0:T(8,128)(2,1)S(1)}, bf16[96,256]{1,0:T(8,128)(2,1)S(1)}, u32[]{:S(2)}, u32[]{:S(2)}) collective-permute-start(bf16[96,256]{1,0:T(8,128)(2,1)S(1)} %pad_maximum_fusion.13), channel_id=1, source_target_pairs={{0,16},{8,24},{16,0},{24,8},{1,17},{9,25},{17,1},{25,9},{2,18},{10... | collective-permute-start | bytes 147464 | tf_op jit(solution)/shard_map/ppermute | solution.py:142
  68.7 2.1 %collective-permute-done.13 = bf16[128,256]{1,0:T(8,128)(2,1)S(1)} collective-permute-done((bf16[128,256]{1,0:T(8,128)(2,1)S(1)}, bf16[128,256]{1,0:T(8,128)(2,1)S(1)}, u32[]{:S(2)}, u32[]{:S(2)}) %collective-permute-start.13) | collective-permute-done | bytes 65568 | tf_op jit(solution)/shard_map/ppermute | solution.py:142
  70.9 1.0 %collective-permute-start.16 = (bf16[96,256]{1,0:T(8,128)(2,1)S(1)}, bf16[96,256]{1,0:T(8,128)(2,1)S(1)}, u32[]{:S(2)}, u32[]{:S(2)}) collective-permute-start(bf16[96,256]{1,0:T(8,128)(2,1)S(1)} %pad_maximum_fusion.14), channel_id=1, source_target_pairs={{0,2},{1,3},{2,0},{3,1},{4,6},{5,7},{6,4},{7,5},{8,10},{9,11},{10,... | collective-permute-start | bytes 147464 | tf_op jit(solution)/shard_map/ppermute | solution.py:142
  71.9 3.1 %collective-permute-done.16 = bf16[96,256]{1,0:T(8,128)(2,1)S(1)} collective-permute-done((bf16[96,256]{1,0:T(8,128)(2,1)S(1)}, bf16[96,256]{1,0:T(8,128)(2,1)S(1)}, u32[]{:S(2)}, u32[]{:S(2)}) %collective-permute-start.16) | collective-permute-done | bytes 49184 | tf_op jit(solution)/shard_map/ppermute | solution.py:142
  75.1 2.4 %collective-permute-start.17 = (bf16[80,256]{1,0:T(8,128)(2,1)S(1)}, bf16[80,256]{1,0:T(8,128)(2,1)S(1)}, u32[]{:S(2)}, u32[]{:S(2)}) collective-permute-start(bf16[80,256]{1,0:T(8,128)(2,1)S(1)} %pad_maximum_fusion.15), channel_id=1, source_target_pairs={{0,4},{1,5},{2,6},{3,7},{4,0},{5,1},{6,2},{7,3},{8,12},{9,13},{10,... | collective-permute-start | bytes 122888 | tf_op jit(solution)/shard_map/ppermute | solution.py:142
  77.5 0.7 fusion.28
  78.2 1.9 %collective-permute-done.17 = bf16[80,256]{1,0:T(8,128)(2,1)S(1)} collective-permute-done((bf16[80,256]{1,0:T(8,128)(2,1)S(1)}, bf16[80,256]{1,0:T(8,128)(2,1)S(1)}, u32[]{:S(2)}, u32[]{:S(2)}) %collective-permute-start.17) | collective-permute-done | bytes 40992 | tf_op jit(solution)/shard_map/ppermute | solution.py:142
  81.4 0.8 %fusion.6 = f32[128,256]{1,0:T(8,128)} fusion(f32[128,256]{1,0:T(8,128)S(1)} %copy-done.5, bf16[64,256]{1,0:T(8,128)(2,1)S(1)} %get-tuple-element.34, bf16[64,256]{1,0:T(8,128)(2,1)S(1)} %get-tuple-element.33, f32[128,256]{1,0:T(8,128)S(1)} %copy-done.4, bf16[64,256]{1,0:T(8,128)(2,1)S(1)} %get-tuple-element.38, bf16[64,256]{1,0:T(8,128)(2,1)S(1)} %get-tuple-element.37, ...), kind=kLoop, calls=%fused_computation.14 | loop fusion | flops 1048576 | bytes 655360 | tf_op jit(solution)/shard_map/sub | solution.py:23
  (99 shorter events, 4.6 us)
Async XLA Ops:
  2.3 6.1 %collective-permute-start = (bf16[3,16,256]{2,1,0:T(8,128)(2,1)}, bf16[3,16,256]{2,1,0:T(8,128)(2,1)S(1)}, u32[]{:S(2)}, u32[]{:S(2)}) collective-permute-start(bf16[3,16,256]{2,1,0:T(8,128)(2,1)} %get-tuple-element.12), channel_id=1, source_target_pairs={{0,4},{1,5},{2,6},{3,7},{4,0},{5,1},{6,2},{7,3},{8,12},{9,13},{10,... | collective-permute-start | bytes 73736 | tf_op jit(solution)/shard_map/ppermute | solution.py:142
  6.3 4.7 %collective-permute-start.3 = (bf16[3,32,256]{2,1,0:T(8,128)(2,1)}, bf16[3,32,256]{2,1,0:T(8,128)(2,1)S(1)}, u32[]{:S(2)}, u32[]{:S(2)}) collective-permute-start(bf16[3,32,256]{2,1,0:T(8,128)(2,1)} %get-tuple-element.13), channel_id=1, source_target_pairs={{0,16},{8,24},{16,0},{24,8},{1,17},{9,25},{17,1},{25,9},{2,18},{10... | collective-permute-start | bytes 147464 | tf_op jit(solution)/shard_map/ppermute | solution.py:142
  9.1 4.2 %collective-permute-start.1 = (bf16[2,3,16,256]{3,2,1,0:T(8,128)(2,1)S(1)}, bf16[2,3,16,256]{3,2,1,0:T(8,128)(2,1)S(1)}, u32[]{:S(2)}, u32[]{:S(2)}) collective-permute-start(bf16[2,3,16,256]{3,2,1,0:T(8,128)(2,1)S(1)} %pad_maximum_fusion.12), channel_id=1, source_target_pairs={{0,2},{1,3},{2,0},{3,1},{4,6},{5,7},{6,4},{7,5},{8,10},{9,11},{10,... | collective-permute-start | bytes 147464 | tf_op jit(solution)/shard_map/ppermute | solution.py:142
  11.9 3.4 %collective-permute-start.4 = (bf16[2,3,32,256]{3,2,1,0:T(8,128)(2,1)S(1)}, bf16[2,3,32,256]{3,2,1,0:T(8,128)(2,1)S(1)}, u32[]{:S(2)}, u32[]{:S(2)}) collective-permute-start(bf16[2,3,32,256]{3,2,1,0:T(8,128)(2,1)S(1)} %pad_maximum_fusion.5), channel_id=1, source_target_pairs={{0,8},{8,0},{16,24},{24,16},{1,9},{9,1},{17,25},{25,17},{2,10},{10... | collective-permute-start | bytes 294920 | tf_op jit(solution)/shard_map/ppermute | solution.py:142
  13.3 4.7 %collective-permute-start.2 = (bf16[2,2,3,16,256]{4,3,2,0,1:T(8,128)(2,1)S(1)}, bf16[2,2,3,16,256]{4,3,2,0,1:T(8,128)(2,1)S(1)}, u32[]{:S(2)}, u32[]{:S(2)}) collective-permute-start(bf16[2,2,3,16,256]{4,3,2,0,1:T(8,128)(2,1)S(1)} %pad_maximum_fusion.4), channel_id=1, source_target_pairs={{0,1},{1,0},{2,3},{3,2},{4,5},{5,4},{6,7},{7,6},{8,9},{9,8},{10,11... | collective-permute-start | bytes 294920 | tf_op jit(solution)/shard_map/ppermute | solution.py:142
  18.1 0.8 %copy-start = (bf16[128,256]{1,0:T(8,128)(2,1)S(1)}, bf16[128,256]{1,0:T(8,128)(2,1)}, u32[]{:S(2)}) copy-start(bf16[128,256]{1,0:T(8,128)(2,1)} %get-tuple-element.14.delay_ref) | copy-start | bytes 196612
  18.9 0.7 copy-start.1
  19.6 33.0 %copy-start.3 = (f32[128,256]{1,0:T(8,128)S(1)}, f32[128,256]{1,0:T(8,128)}, u32[]{:S(2)}) copy-start(f32[128,256]{1,0:T(8,128)} %refs_6_.1) | copy-start | bytes 393220
  19.6 33.0 %copy-start.4 = (f32[128,256]{1,0:T(8,128)S(1)}, f32[128,256]{1,0:T(8,128)}, u32[]{:S(2)}) copy-start(f32[128,256]{1,0:T(8,128)} %param.23) | copy-start | bytes 393220
  19.6 33.1 %copy-start.5 = (f32[128,256]{1,0:T(8,128)S(1)}, f32[128,256]{1,0:T(8,128)}, u32[]{:S(2)}) copy-start(f32[128,256]{1,0:T(8,128)} %param.22) | copy-start | bytes 393220
  19.6 33.2 %copy-start.2 = (f32[8]{0:T(128)S(1)}, f32[8]{0:T(128)}, u32[]{:S(2)}) copy-start(f32[8]{0:T(128)} %prop_ref.3) | copy-start | bytes 100
  30.3 1.4 %collective-permute-start.5 = (bf16[192,256]{1,0:T(8,128)(2,1)S(1)}, bf16[192,256]{1,0:T(8,128)(2,1)S(1)}, u32[]{:S(2)}, u32[]{:S(2)}) collective-permute-start(bf16[192,256]{1,0:T(8,128)(2,1)S(1)} %pad_maximum_fusion.6), channel_id=1, source_target_pairs={{0,8},{8,0},{16,24},{24,16},{1,9},{9,1},{17,25},{25,17},{2,10},{10... | collective-permute-start | bytes 294920 | tf_op jit(solution)/shard_map/ppermute | solution.py:142
  31.7 4.9 %collective-permute-start.8 = (bf16[64,256]{1,0:T(8,128)(2,1)S(1)}, bf16[64,256]{1,0:T(8,128)(2,1)S(1)}, u32[]{:S(2)}, u32[]{:S(2)}) collective-permute-start(bf16[64,256]{1,0:T(8,128)(2,1)S(1)} %add_convert_fusion.12), channel_id=1, source_target_pairs={{0,17},{1,16},{2,19},{3,18},{4,21},{5,20},{6,23},{7,22},{8,25},{9,... | collective-permute-start | bytes 98312 | tf_op jit(solution)/shard_map/ppermute | solution.py:166
  34.7 4.7 %collective-permute-start.6 = (bf16[192,256]{1,0:T(8,128)(2,1)S(1)}, bf16[192,256]{1,0:T(8,128)(2,1)S(1)}, u32[]{:S(2)}, u32[]{:S(2)}) collective-permute-start(bf16[192,256]{1,0:T(8,128)(2,1)S(1)} %get-tuple-element.42), channel_id=1, source_target_pairs={{0,1},{1,0},{2,3},{3,2},{4,5},{5,4},{6,7},{7,6},{8,9},{9,8},{10,11... | collective-permute-start | bytes 294920 | tf_op jit(solution)/shard_map/ppermute | solution.py:142
  35.3 4.6 %collective-permute-start.7 = (bf16[192,256]{1,0:T(8,128)(2,1)S(1)}, bf16[192,256]{1,0:T(8,128)(2,1)S(1)}, u32[]{:S(2)}, u32[]{:S(2)}) collective-permute-start(bf16[192,256]{1,0:T(8,128)(2,1)S(1)} %get-tuple-element.41), channel_id=1, source_target_pairs={{0,16},{8,24},{16,0},{24,8},{1,17},{9,25},{17,1},{25,9},{2,18},{10... | collective-permute-start | bytes 294920 | tf_op jit(solution)/shard_map/ppermute | solution.py:142
  39.9 4.7 %collective-permute-start.9 = (bf16[192,256]{1,0:T(8,128)(2,1)S(1)}, bf16[192,256]{1,0:T(8,128)(2,1)S(1)}, u32[]{:S(2)}, u32[]{:S(2)}) collective-permute-start(bf16[192,256]{1,0:T(8,128)(2,1)S(1)} %pad_maximum_fusion.7), channel_id=1, source_target_pairs={{0,2},{1,3},{2,0},{3,1},{4,6},{5,7},{6,4},{7,5},{8,10},{9,11},{10,... | collective-permute-start | bytes 294920 | tf_op jit(solution)/shard_map/ppermute | solution.py:142
  44.7 6.6 %collective-permute-start.10 = (bf16[192,256]{1,0:T(8,128)(2,1)S(1)}, bf16[192,256]{1,0:T(8,128)(2,1)S(1)}, u32[]{:S(2)}, u32[]{:S(2)}) collective-permute-start(bf16[192,256]{1,0:T(8,128)(2,1)S(1)} %pad_maximum_fusion.8), channel_id=1, source_target_pairs={{0,4},{1,5},{2,6},{3,7},{4,0},{5,1},{6,2},{7,3},{8,12},{9,13},{10,... | collective-permute-start | bytes 294920 | tf_op jit(solution)/shard_map/ppermute | solution.py:142
  51.3 1.3 %collective-permute-start.11 = (bf16[64,256]{1,0:T(8,128)(2,1)S(1)}, bf16[64,256]{1,0:T(8,128)(2,1)S(1)}, u32[]{:S(2)}, u32[]{:S(2)}) collective-permute-start(bf16[64,256]{1,0:T(8,128)(2,1)S(1)} %add_convert_fusion.9), channel_id=1, source_target_pairs={{0,8},{8,0},{16,24},{24,16},{1,9},{9,1},{17,25},{25,17},{2,10},{10... | collective-permute-start | bytes 98312 | tf_op jit(solution)/shard_map/ppermute | solution.py:142
  51.4 26.1 %copy-start.6 = (f32[32,256]{1,0:T(8,128)S(1)}, f32[32,256]{1,0:T(8,128)}, u32[]{:S(2)}) copy-start(f32[32,256]{1,0:T(8,128)} %refs_3_.1) | copy-start | bytes 98308
  51.5 26.1 %copy-start.7 = (f32[32,256]{1,0:T(8,128)S(1)}, f32[32,256]{1,0:T(8,128)}, u32[]{:S(2)}) copy-start(f32[32,256]{1,0:T(8,128)} %refs_4_.1) | copy-start | bytes 98308
  51.5 26.0 %copy-start.8 = (f32[32,256]{1,0:T(8,128)S(1)}, f32[32,256]{1,0:T(8,128)}, u32[]{:S(2)}) copy-start(f32[32,256]{1,0:T(8,128)} %refs_5_.1) | copy-start | bytes 98308
  51.5 28.7 %copy-start.9 = (f32[16,256]{1,0:T(8,128)S(1)}, f32[16,256]{1,0:T(8,128)}, u32[]{:S(2)}) copy-start(f32[16,256]{1,0:T(8,128)} %refs_0_.1) | copy-start | bytes 49156
  51.5 28.7 %copy-start.10 = (f32[16,256]{1,0:T(8,128)S(1)}, f32[16,256]{1,0:T(8,128)}, u32[]{:S(2)}) copy-start(f32[16,256]{1,0:T(8,128)} %refs_1_.1) | copy-start | bytes 49156
  51.5 28.7 %copy-start.11 = (f32[16,256]{1,0:T(8,128)S(1)}, f32[16,256]{1,0:T(8,128)}, u32[]{:S(2)}) copy-start(f32[16,256]{1,0:T(8,128)} %refs_2_.1) | copy-start | bytes 49156
  63.7 1.3 %collective-permute-start.12 = (bf16[128,256]{1,0:T(8,128)(2,1)S(1)}, bf16[128,256]{1,0:T(8,128)(2,1)S(1)}, u32[]{:S(2)}, u32[]{:S(2)}) collective-permute-start(bf16[128,256]{1,0:T(8,128)(2,1)S(1)} %pad_maximum_fusion.10), channel_id=1, source_target_pairs={{0,8},{8,0},{16,24},{24,16},{1,9},{9,1},{17,25},{25,17},{2,10},{10... | collective-permute-start | bytes 196616 | tf_op jit(solution)/shard_map/ppermute | solution.py:142
  65.0 5.8 %collective-permute-start.15 = (bf16[64,256]{1,0:T(8,128)(2,1)S(1)}, bf16[64,256]{1,0:T(8,128)(2,1)S(1)}, u32[]{:S(2)}, u32[]{:S(2)}) collective-permute-start(bf16[64,256]{1,0:T(8,128)(2,1)S(1)} %add_convert_fusion.8), channel_id=1, source_target_pairs={{0,17},{1,16},{2,19},{3,18},{4,21},{5,20},{6,23},{7,22},{8,25},{9,... | collective-permute-start | bytes 98312 | tf_op jit(solution)/shard_map/ppermute | solution.py:166
  66.5 4.3 %collective-permute-start.13 = (bf16[128,256]{1,0:T(8,128)(2,1)S(1)}, bf16[128,256]{1,0:T(8,128)(2,1)S(1)}, u32[]{:S(2)}, u32[]{:S(2)}) collective-permute-start(bf16[128,256]{1,0:T(8,128)(2,1)S(1)} %pad_maximum_fusion.11), channel_id=1, source_target_pairs={{0,1},{1,0},{2,3},{3,2},{4,5},{5,4},{6,7},{7,6},{8,9},{9,8},{10,11... | collective-permute-start | bytes 196616 | tf_op jit(solution)/shard_map/ppermute | solution.py:142
  66.7 4.2 %collective-permute-start.14 = (bf16[96,256]{1,0:T(8,128)(2,1)S(1)}, bf16[96,256]{1,0:T(8,128)(2,1)S(1)}, u32[]{:S(2)}, u32[]{:S(2)}) collective-permute-start(bf16[96,256]{1,0:T(8,128)(2,1)S(1)} %pad_maximum_fusion.13), channel_id=1, source_target_pairs={{0,16},{8,24},{16,0},{24,8},{1,17},{9,25},{17,1},{25,9},{2,18},{10... | collective-permute-start | bytes 147464 | tf_op jit(solution)/shard_map/ppermute | solution.py:142
  70.9 4.2 %collective-permute-start.16 = (bf16[96,256]{1,0:T(8,128)(2,1)S(1)}, bf16[96,256]{1,0:T(8,128)(2,1)S(1)}, u32[]{:S(2)}, u32[]{:S(2)}) collective-permute-start(bf16[96,256]{1,0:T(8,128)(2,1)S(1)} %pad_maximum_fusion.14), channel_id=1, source_target_pairs={{0,2},{1,3},{2,0},{3,1},{4,6},{5,7},{6,4},{7,5},{8,10},{9,11},{10,... | collective-permute-start | bytes 147464 | tf_op jit(solution)/shard_map/ppermute | solution.py:142
  75.1 5.0 %collective-permute-start.17 = (bf16[80,256]{1,0:T(8,128)(2,1)S(1)}, bf16[80,256]{1,0:T(8,128)(2,1)S(1)}, u32[]{:S(2)}, u32[]{:S(2)}) collective-permute-start(bf16[80,256]{1,0:T(8,128)(2,1)S(1)} %pad_maximum_fusion.15), channel_id=1, source_target_pairs={{0,4},{1,5},{2,6},{3,7},{4,0},{5,1},{6,2},{7,3},{8,12},{9,13},{10,... | collective-permute-start | bytes 122888 | tf_op jit(solution)/shard_map/ppermute | solution.py:142
  80.1 1.3 %collective-permute-start.18 = (bf16[64,256]{1,0:T(8,128)(2,1)S(1)}, bf16[64,256]{1,0:T(8,128)(2,1)S(1)}, u32[]{:S(2)}, u32[]{:S(2)}) collective-permute-start(bf16[64,256]{1,0:T(8,128)(2,1)S(1)} %add_convert_fusion.5), channel_id=1, source_target_pairs={{0,8},{8,0},{16,24},{24,16},{1,9},{9,1},{17,25},{25,17},{2,10},{10... | collective-permute-start | bytes 98312 | tf_op jit(solution)/shard_map/ppermute | solution.py:142

commit v3 on v2

--- a/solution.py
+++ b/solution.py
@@ -24,44 +24,31 @@
     return (factor, moment, second)
 
 
-def grads_kernel(
-    prop_ref, obs_hbm, bucket_hbm, camp_ref, hour_ref, delay_ref,
-    ga_ref, gb_ref, gc_ref, gb_sum, gc_sum, obs_ref, bucket_ref, sems,
+def fill_table(table_ref, prop_ref):
+    lane = lax.broadcasted_iota(jnp.int32, table_ref.shape, 1)
+    chance = jnp.ones(table_ref.shape, F32)
+    for level in range(prop_ref.shape[0]):
+        chance = jnp.where(lane == level + 1, prop_ref[level], chance)
+    table_ref[...] = jnp.where(lane == 0, 0.0, 1.0 / chance)
+
+
+def tile_gradients(
+    table_ref, obs_ref, bucket_ref, camp_ref, hour_ref, delay_ref,
+    ga_ref, gb_ref, gc_ref, gb_sum, gc_sum, parts, arrived,
 ):
     total, cols, delays = obs_ref.shape
     rank = hour_ref.shape[1]
-    parts = sems.shape[1]
     rows = total // parts
     sub = math.gcd(rows, 8)
     flat = sub * cols
-
-    def fetches(part):
-        at = pl.ds(part * rows, rows)
-        return (
-            pltpu.make_async_copy(obs_hbm.at[at], obs_ref.at[at], sems.at[0, part]),
-            pltpu.make_async_copy(bucket_hbm.at[at], bucket_ref.at[at], sems.at[1, part]),
-        )
-
-    for part in range(parts):
-        for fetch in fetches(part):
-            fetch.start()
-
     gb_sum[...] = jnp.zeros_like(gb_sum)
     gc_sum[...] = jnp.zeros_like(gc_sum)
-    lane = lax.broadcasted_iota(jnp.int32, (8, delays), 1)
-    chance = jnp.ones((8, delays), F32)
-    for level in range(prop_ref.shape[0]):
-        chance = jnp.where(lane == level + 1, prop_ref[level], chance)
-    table = jnp.where(lane == 0, 0.0, 1.0 / chance)
-    table = jnp.broadcast_to(table[:1], (flat, delays))
-
     hour16 = hour_ref[...]
     hour = hour16.astype(F32)
     delay = delay_ref[...]
-
     for part in range(parts):
-        for fetch in fetches(part):
-            fetch.wait()
+        arrived(part)
+        table = jnp.broadcast_to(table_ref[:1], (flat, delays))
         gb_part, gc_part = gb_sum[...], gc_sum[...]
         for start in range(part * rows, (part + 1) * rows, sub):
             camp = camp_ref[start:start + sub]
@@ -81,17 +68,57 @@
     gc_ref[...] = gc_sum[...].astype(gc_ref.dtype)
 
 
+AHEAD = 3
+
+
+def grads_kernel(
+    prop_hbm, obs_hbm, bucket_hbm, camp_ref, hour_ref, delay_ref,
+    ga_ref, gb_ref, gc_ref,
+    gb_sum, gc_sum, table_ref, obs_ref, bucket_ref, prop_ref, prop_sem, sems,
+):
+    parts = sems.shape[1]
+    rows = obs_ref.shape[0] // parts
+
+    def fetches(part):
+        at = pl.ds(part * rows, rows)
+        return (
+            pltpu.make_async_copy(obs_hbm.at[at], obs_ref.at[at], sems.at[0, part]),
+            pltpu.make_async_copy(bucket_hbm.at[at], bucket_ref.at[at], sems.at[1, part]),
+        )
+
+    def begin(part):
+        if part < parts:
+            for fetch in fetches(part):
+                fetch.start()
+
+    def arrived(part):
+        begin(part + AHEAD)
+        for fetch in fetches(part):
+            fetch.wait()
+
+    prop_fetch = pltpu.make_async_copy(prop_hbm, prop_ref, prop_sem)
+    prop_fetch.start()
+    for part in range(AHEAD):
+        begin(part)
+    prop_fetch.wait()
+    fill_table(table_ref, prop_ref)
+    tile_gradients(
+        table_ref, obs_ref, bucket_ref, camp_ref, hour_ref, delay_ref,
+        ga_ref, gb_ref, gc_ref, gb_sum, gc_sum, parts, arrived,
+    )
+
+
 def gradients(propensity, observed, bucket, camp_block, hour_block, delay_block):
     tile_rows, tile_cols, delay_count = observed.shape
     rank = camp_block.shape[1]
     parts = tile_rows // math.gcd(tile_rows, 16)
     vmem = pl.BlockSpec(memory_space=pltpu.VMEM)
     hbm = pl.BlockSpec(memory_space=pltpu.HBM)
-    observed, bucket = (pltpu.with_memory_space_constraint(x, pltpu.HBM) for x in (observed, bucket))
+    large = [pltpu.with_memory_space_constraint(x, pltpu.HBM) for x in (propensity, observed, bucket)]
     return pl.pallas_call(
         grads_kernel,
-        in_specs=[pl.BlockSpec(memory_space=pltpu.SMEM), hbm, hbm, vmem, vmem, vmem],
-        out_specs=[vmem, vmem, vmem],
+        in_specs=[hbm] * 3 + [vmem] * 3,
+        out_specs=[vmem] * 3,
         out_shape=[
             jax.ShapeDtypeStruct((tile_rows, rank), F32),
             jax.ShapeDtypeStruct((tile_cols, rank), BF16),
@@ -100,8 +127,11 @@
         scratch_shapes=[
             pltpu.VMEM((tile_cols, rank), F32),
             pltpu.VMEM((delay_count, rank), F32),
+            pltpu.VMEM((8, delay_count), F32),
             pltpu.VMEM(observed.shape, observed.dtype),
             pltpu.VMEM(bucket.shape, bucket.dtype),
+            pltpu.SMEM(propensity.shape, F32),
+            pltpu.SemaphoreType.DMA,
             pltpu.SemaphoreType.DMA((2, parts)),
         ],
         compiler_params=pltpu.CompilerParams(vmem_limit_bytes=40 * 1024 * 1024),
@@ -111,7 +141,7 @@
             transcendentals=0,
         ),
         name="gradients",
-    )(propensity, observed, bucket, camp_block, hour_block, delay_block)
+    )(*large, camp_block, hour_block, delay_block)
 
 
 def pack_kernel(*refs):
@@ -124,6 +154,7 @@
 
 def pack(camp, hour, delay):
     vmem = pl.BlockSpec(memory_space=pltpu.VMEM)
+    arrays = [pltpu.with_memory_space_constraint(x, pltpu.HBM) for x in (*camp, *hour, delay)]
     return pl.pallas_call(
         pack_kernel,
         in_specs=[vmem] * 7,
@@ -133,8 +164,9 @@
             jax.ShapeDtypeStruct((3,) + hour[0].shape, BF16),
             jax.ShapeDtypeStruct(delay.shape, BF16),
         ],
+        compiler_params=pltpu.CompilerParams(vmem_limit_bytes=8 * 1024 * 1024),
         name="pack",
-    )(*camp, *hour, delay)
+    )(*arrays)
 
 
 def swap(block, axis, bit):

time: 82.5 us -> 78.4 us (0.950)
  Pallas kernels: 23.1 us -> 21.4 us
  other arithmetic: 4.66 us -> 3.13 us
  local copies, waits for them, and re-layouts: 1.61 us -> 0.12 us
    another operation x10, other arithmetic: 1.68 us -> 0.15 us  [gather_blocks(): block = jnp.stack([low_block, high_block], axis=depth)]
    unnamed x24 -> x18, local copies, waits for them, and re-layouts: 1.54 us -> 0.06 us
    pallas_call x2, Pallas kernels: 21.4 us -> 20.4 us  [gradients(): pl.pallas_call(grads_kernel, in_specs=[hbm] * 3 + [vmem] * 3, out_specs=[...]
  transfers between devices with their start and end apart: 19 -> 19, of which waited for: 15 -> 16; matrix products, arithmetic and copies ran while one was open for 4% -> 2% of each run, Pallas kernels for 0% -> 0%
where the time goes in v3:
time: 78.4 us; the launch traced here: 78.2 us
  waiting for transfers between devices  27.6 us (35%)
  starting transfers between devices  24.7 us (32%)
  Pallas kernels  21.4 us (27%)
  other arithmetic  3.13 us (4%)
  between operations  1.17 us (1%)
    ppermute x17, waiting for transfers between devices, swap(): return lax.ppermute(block, axis, [(i, i ^ bit) for i in range(size)])  26.4 us
    pallas_call x2, Pallas kernels, gradients(): pl.pallas_call(grads_kernel, in_specs=[hbm] * 3 + [vmem] * 3, out_specs=[...  20.4 us
    ppermute x17, starting transfers between devices, swap(): return lax.ppermute(block, axis, [(i, i ^ bit) for i in range(size)])  20.3 us
    ppermute x2, starting transfers between devices, swap_both(): lax.ppermute(block, ('camp', 'hour'), [(i, i ^ camp_bit * hours + hour_bi...  4.5 us
    sub x3, other arithmetic, adam_update(): factor = factor - learn_rate * moment / (jnp.sqrt(second) + adam_eps)  2.17 us
  transfers between devices with their start and end apart: 19, of which 16 were waited for; matrix products, arithmetic and copies ran while one was open for 2% of the time, Pallas kernels for 0%

profile of v3, /device:TPU:0, one launch (start us, length us, event | category | flops | bytes accessed | tf_op | source)
XLA Modules:
  0.0 78.2 jit_solution(14889191081396992075)
XLA Ops:
  0.6 1.0 %pack.1 = (bf16[3,16,256]{2,1,0:T(8,128)(2,1)S(1)}, bf16[3,32,256]{2,1,0:T(8,128)(2,1)S(1)}, bf16[128,256]{1,0:T(8,128)(2,1)S(1)}) custom-call(f32[16,256]{1,0:T(8,128)} %refs_0_.1, f32[16,256]{1,0:T(8,128)} %refs_1_.1, f32[16,256]{1,0:T(8,128)} %refs_2_.1, f32[32,256]{1,0:T(8,128)} %refs_3_.1, f32[32,256]{1,0:T(8,128)} %refs_4_.1, f32[32,256]{1,0:T(8,128)} %refs_5_.1, ...), custom_call_target="tpu_custom_call" | custom-call | tf_op jit(solution)/shard_map/pack/pallas_call | solution.py:158
  1.7 4.1 %collective-permute-start = (bf16[3,16,256]{2,1,0:T(8,128)(2,1)S(1)}, bf16[3,16,256]{2,1,0:T(8,128)(2,1)S(1)}, u32[]{:S(2)}, u32[]{:S(2)}) collective-permute-start(bf16[3,16,256]{2,1,0:T(8,128)(2,1)S(1)} %get-tuple-element.12), channel_id=1, source_target_pairs={{0,4},{1,5},{2,6},{3,7},{4,0},{5,1},{6,2},{7,3},{8,12},{9,13},{10,... | collective-permute-start | bytes 73736 | tf_op jit(solution)/shard_map/ppermute | solution.py:174
  5.8 1.5 %collective-permute-start.3 = (bf16[3,32,256]{2,1,0:T(8,128)(2,1)S(1)}, bf16[3,32,256]{2,1,0:T(8,128)(2,1)S(1)}, u32[]{:S(2)}, u32[]{:S(2)}) collective-permute-start(bf16[3,32,256]{2,1,0:T(8,128)(2,1)S(1)} %get-tuple-element.13), channel_id=1, source_target_pairs={{0,16},{8,24},{16,0},{24,8},{1,17},{9,25},{17,1},{25,9},{2,18},{10... | collective-permute-start | bytes 147464 | tf_op jit(solution)/shard_map/ppermute | solution.py:174
  7.6 2.0 %collective-permute-start.1 = (bf16[2,3,16,256]{3,2,1,0:T(8,128)(2,1)S(1)}, bf16[2,3,16,256]{3,2,1,0:T(8,128)(2,1)S(1)}, u32[]{:S(2)}, u32[]{:S(2)}) collective-permute-start(bf16[2,3,16,256]{3,2,1,0:T(8,128)(2,1)S(1)} %pad_maximum_fusion.12), channel_id=1, source_target_pairs={{0,2},{1,3},{2,0},{3,1},{4,6},{5,7},{6,4},{7,5},{8,10},{9,11},{10,... | collective-permute-start | bytes 147464 | tf_op jit(solution)/shard_map/ppermute | solution.py:174
  10.0 1.8 %collective-permute-done.1 = bf16[2,3,16,256]{3,2,1,0:T(8,128)(2,1)S(1)} collective-permute-done((bf16[2,3,16,256]{3,2,1,0:T(8,128)(2,1)S(1)}, bf16[2,3,16,256]{3,2,1,0:T(8,128)(2,1)S(1)}, u32[]{:S(2)}, u32[]{:S(2)}) %collective-permute-start.1) | collective-permute-done | bytes 49184 | tf_op jit(solution)/shard_map/ppermute | solution.py:174
  11.8 2.0 %collective-permute-start.2 = (bf16[2,2,3,16,256]{4,3,2,0,1:T(8,128)(2,1)S(1)}, bf16[2,2,3,16,256]{4,3,2,0,1:T(8,128)(2,1)S(1)}, u32[]{:S(2)}, u32[]{:S(2)}) collective-permute-start(bf16[2,2,3,16,256]{4,3,2,0,1:T(8,128)(2,1)S(1)} %pad_maximum_fusion.4), channel_id=1, source_target_pairs={{0,1},{1,0},{2,3},{3,2},{4,5},{5,4},{6,7},{7,6},{8,9},{9,8},{10,11... | collective-permute-start | bytes 294920 | tf_op jit(solution)/shard_map/ppermute | solution.py:174
  13.9 2.6 %collective-permute-done.2 = bf16[2,2,3,16,256]{4,3,2,0,1:T(8,128)(2,1)S(1)} collective-permute-done((bf16[2,2,3,16,256]{4,3,2,0,1:T(8,128)(2,1)S(1)}, bf16[2,2,3,16,256]{4,3,2,0,1:T(8,128)(2,1)S(1)}, u32[]{:S(2)}, u32[]{:S(2)}) %collective-permute-start.2) | collective-permute-done | bytes 98336 | tf_op jit(solution)/shard_map/ppermute | solution.py:174
  16.6 10.1 %gradients.2 = (f32[128,256]{1,0:T(8,128)S(1)}, bf16[128,256]{1,0:T(8,128)(2,1)S(1)}, bf16[128,256]{1,0:T(8,128)(2,1)S(1)}) custom-call(f32[8]{0:T(128)} %prop_hbm.3, bf16[128,128,128]{2,1,0:T(8,128)(2,1)} %obs_hbm.3, s32[128,128,128]{2,1,0:T(8,128)} %bucket_hbm.3, bf16[128,256]{1,0:T(8,128)(2,1)S(1)} %bitcast.109, bf16[128,256]{1,0:T(8,128)(2,1)S(1)} %bitcast.108, ...), custom_call_target="tpu_custom_call" | custom-call | flops 3221225472 | bytes 12582912 | tf_op jit(solution)/shard_map/gradients/pallas_call | solution.py:118
  26.9 1.3 %collective-permute-done.5 = bf16[192,256]{1,0:T(8,128)(2,1)S(1)} collective-permute-done((bf16[192,256]{1,0:T(8,128)(2,1)S(1)}, bf16[192,256]{1,0:T(8,128)(2,1)S(1)}, u32[]{:S(2)}, u32[]{:S(2)}) %collective-permute-start.5) | collective-permute-done | bytes 98336 | tf_op jit(solution)/shard_map/ppermute | solution.py:174
  28.2 3.0 %collective-permute-start.8 = (bf16[64,256]{1,0:T(8,128)(2,1)S(1)}, bf16[64,256]{1,0:T(8,128)(2,1)S(1)}, u32[]{:S(2)}, u32[]{:S(2)}) collective-permute-start(bf16[64,256]{1,0:T(8,128)(2,1)S(1)} %add_convert_fusion.12), channel_id=1, source_target_pairs={{0,17},{1,16},{2,19},{3,18},{4,21},{5,20},{6,23},{7,22},{8,25},{9,... | collective-permute-start | bytes 98312 | tf_op jit(solution)/shard_map/ppermute | solution.py:198
  31.2 0.6 collective-permute-start.6
  31.9 1.2 %collective-permute-done.8 = bf16[64,256]{1,0:T(8,128)(2,1)S(1)} collective-permute-done((bf16[64,256]{1,0:T(8,128)(2,1)S(1)}, bf16[64,256]{1,0:T(8,128)(2,1)S(1)}, u32[]{:S(2)}, u32[]{:S(2)}) %collective-permute-start.8) | collective-permute-done | bytes 32800 | tf_op jit(solution)/shard_map/ppermute | solution.py:198
  33.1 2.8 %collective-permute-done.6 = bf16[192,256]{1,0:T(8,128)(2,1)S(1)} collective-permute-done((bf16[192,256]{1,0:T(8,128)(2,1)S(1)}, bf16[192,256]{1,0:T(8,128)(2,1)S(1)}, u32[]{:S(2)}, u32[]{:S(2)}) %collective-permute-start.6) | collective-permute-done | bytes 98336 | tf_op jit(solution)/shard_map/ppermute | solution.py:174
  35.9 0.5 collective-permute-done.7
  36.5 1.5 %collective-permute-start.9 = (bf16[192,256]{1,0:T(8,128)(2,1)S(1)}, bf16[192,256]{1,0:T(8,128)(2,1)S(1)}, u32[]{:S(2)}, u32[]{:S(2)}) collective-permute-start(bf16[192,256]{1,0:T(8,128)(2,1)S(1)} %pad_maximum_fusion.7), channel_id=1, source_target_pairs={{0,2},{1,3},{2,0},{3,1},{4,6},{5,7},{6,4},{7,5},{8,10},{9,11},{10,... | collective-permute-start | bytes 294920 | tf_op jit(solution)/shard_map/ppermute | solution.py:174
  38.0 3.2 %collective-permute-done.9 = bf16[192,256]{1,0:T(8,128)(2,1)S(1)} collective-permute-done((bf16[192,256]{1,0:T(8,128)(2,1)S(1)}, bf16[192,256]{1,0:T(8,128)(2,1)S(1)}, u32[]{:S(2)}, u32[]{:S(2)}) %collective-permute-start.9) | collective-permute-done | bytes 98336 | tf_op jit(solution)/shard_map/ppermute | solution.py:174
  41.2 2.5 %collective-permute-start.10 = (bf16[192,256]{1,0:T(8,128)(2,1)S(1)}, bf16[192,256]{1,0:T(8,128)(2,1)S(1)}, u32[]{:S(2)}, u32[]{:S(2)}) collective-permute-start(bf16[192,256]{1,0:T(8,128)(2,1)S(1)} %pad_maximum_fusion.8), channel_id=1, source_target_pairs={{0,4},{1,5},{2,6},{3,7},{4,0},{5,1},{6,2},{7,3},{8,12},{9,13},{10,... | collective-permute-start | bytes 294920 | tf_op jit(solution)/shard_map/ppermute | solution.py:174
  43.8 4.1 %collective-permute-done.10 = bf16[192,256]{1,0:T(8,128)(2,1)S(1)} collective-permute-done((bf16[192,256]{1,0:T(8,128)(2,1)S(1)}, bf16[192,256]{1,0:T(8,128)(2,1)S(1)}, u32[]{:S(2)}, u32[]{:S(2)}) %collective-permute-start.10) | collective-permute-done | bytes 98336 | tf_op jit(solution)/shard_map/ppermute | solution.py:174
  48.3 0.9 %collective-permute-done.11 = bf16[64,256]{1,0:T(8,128)(2,1)S(1)} collective-permute-done((bf16[64,256]{1,0:T(8,128)(2,1)S(1)}, bf16[64,256]{1,0:T(8,128)(2,1)S(1)}, u32[]{:S(2)}, u32[]{:S(2)}) %collective-permute-start.11) | collective-permute-done | bytes 32800 | tf_op jit(solution)/shard_map/ppermute | solution.py:174
  49.3 10.3 %gradients.3 = (f32[128,256]{1,0:T(8,128)S(1)}, bf16[128,256]{1,0:T(8,128)(2,1)S(1)}, bf16[128,256]{1,0:T(8,128)(2,1)S(1)}) custom-call(f32[8]{0:T(128)} %prop_hbm.3, bf16[128,128,128]{2,1,0:T(8,128)(2,1)} %obs_hbm.3, s32[128,128,128]{2,1,0:T(8,128)} %bucket_hbm.3, bf16[128,256]{1,0:T(8,128)(2,1)S(1)} %get-tuple-element.43.camp_ref, ...), custom_call_target="tpu_custom_call" | custom-call | flops 3221225472 | bytes 12582912 | tf_op jit(solution)/shard_map/gradients/pallas_call | solution.py:118
  59.9 1.1 %collective-permute-done.12 = bf16[128,256]{1,0:T(8,128)(2,1)S(1)} collective-permute-done((bf16[128,256]{1,0:T(8,128)(2,1)S(1)}, bf16[128,256]{1,0:T(8,128)(2,1)S(1)}, u32[]{:S(2)}, u32[]{:S(2)}) %collective-permute-start.12) | collective-permute-done | bytes 65568 | tf_op jit(solution)/shard_map/ppermute | solution.py:174
  61.0 1.5 %collective-permute-start.15 = (bf16[64,256]{1,0:T(8,128)(2,1)S(1)}, bf16[64,256]{1,0:T(8,128)(2,1)S(1)}, u32[]{:S(2)}, u32[]{:S(2)}) collective-permute-start(bf16[64,256]{1,0:T(8,128)(2,1)S(1)} %add_convert_fusion.8), channel_id=1, source_target_pairs={{0,17},{1,16},{2,19},{3,18},{4,21},{5,20},{6,23},{7,22},{8,25},{9,... | collective-permute-start | bytes 98312 | tf_op jit(solution)/shard_map/ppermute | solution.py:198
  62.7 2.0 %collective-permute-start.14 = (bf16[96,256]{1,0:T(8,128)(2,1)S(1)}, bf16[96,256]{1,0:T(8,128)(2,1)S(1)}, u32[]{:S(2)}, u32[]{:S(2)}) collective-permute-start(bf16[96,256]{1,0:T(8,128)(2,1)S(1)} %pad_maximum_fusion.13), channel_id=1, source_target_pairs={{0,16},{8,24},{16,0},{24,8},{1,17},{9,25},{17,1},{25,9},{2,18},{10... | collective-permute-start | bytes 147464 | tf_op jit(solution)/shard_map/ppermute | solution.py:174
  64.7 2.1 %collective-permute-done.13 = bf16[128,256]{1,0:T(8,128)(2,1)S(1)} collective-permute-done((bf16[128,256]{1,0:T(8,128)(2,1)S(1)}, bf16[128,256]{1,0:T(8,128)(2,1)S(1)}, u32[]{:S(2)}, u32[]{:S(2)}) %collective-permute-start.13) | collective-permute-done | bytes 65568 | tf_op jit(solution)/shard_map/ppermute | solution.py:174
  66.9 1.0 %collective-permute-start.16 = (bf16[96,256]{1,0:T(8,128)(2,1)S(1)}, bf16[96,256]{1,0:T(8,128)(2,1)S(1)}, u32[]{:S(2)}, u32[]{:S(2)}) collective-permute-start(bf16[96,256]{1,0:T(8,128)(2,1)S(1)} %pad_maximum_fusion.14), channel_id=1, source_target_pairs={{0,2},{1,3},{2,0},{3,1},{4,6},{5,7},{6,4},{7,5},{8,10},{9,11},{10,... | collective-permute-start | bytes 147464 | tf_op jit(solution)/shard_map/ppermute | solution.py:174
  67.9 3.1 %collective-permute-done.16 = bf16[96,256]{1,0:T(8,128)(2,1)S(1)} collective-permute-done((bf16[96,256]{1,0:T(8,128)(2,1)S(1)}, bf16[96,256]{1,0:T(8,128)(2,1)S(1)}, u32[]{:S(2)}, u32[]{:S(2)}) %collective-permute-start.16) | collective-permute-done | bytes 49184 | tf_op jit(solution)/shard_map/ppermute | solution.py:174
  71.1 2.4 %collective-permute-start.17 = (bf16[80,256]{1,0:T(8,128)(2,1)S(1)}, bf16[80,256]{1,0:T(8,128)(2,1)S(1)}, u32[]{:S(2)}, u32[]{:S(2)}) collective-permute-start(bf16[80,256]{1,0:T(8,128)(2,1)S(1)} %pad_maximum_fusion.15), channel_id=1, source_target_pairs={{0,4},{1,5},{2,6},{3,7},{4,0},{5,1},{6,2},{7,3},{8,12},{9,13},{10,... | collective-permute-start | bytes 122888 | tf_op jit(solution)/shard_map/ppermute | solution.py:174
  73.5 0.7 fusion.28
  74.2 1.9 %collective-permute-done.17 = bf16[80,256]{1,0:T(8,128)(2,1)S(1)} collective-permute-done((bf16[80,256]{1,0:T(8,128)(2,1)S(1)}, bf16[80,256]{1,0:T(8,128)(2,1)S(1)}, u32[]{:S(2)}, u32[]{:S(2)}) %collective-permute-start.17) | collective-permute-done | bytes 40992 | tf_op jit(solution)/shard_map/ppermute | solution.py:174
  76.2 0.6 fusion.38
  76.9 0.5 collective-permute-done.18
  77.4 0.8 %fusion.6 = f32[128,256]{1,0:T(8,128)} fusion(f32[128,256]{1,0:T(8,128)S(1)} %copy-done.2, bf16[64,256]{1,0:T(8,128)(2,1)S(1)} %get-tuple-element.34, bf16[64,256]{1,0:T(8,128)(2,1)S(1)} %get-tuple-element.33, f32[128,256]{1,0:T(8,128)S(1)} %copy-done.1, bf16[64,256]{1,0:T(8,128)(2,1)S(1)} %get-tuple-element.38, bf16[64,256]{1,0:T(8,128)(2,1)S(1)} %get-tuple-element.37, ...), kind=kLoop, calls=%fused_computation.14 | loop fusion | flops 1048576 | bytes 655360 | tf_op jit(solution)/shard_map/sub | solution.py:23
  (93 shorter events, 2.3 us)
Async XLA Ops:
  1.7 5.9 %collective-permute-start = (bf16[3,16,256]{2,1,0:T(8,128)(2,1)S(1)}, bf16[3,16,256]{2,1,0:T(8,128)(2,1)S(1)}, u32[]{:S(2)}, u32[]{:S(2)}) collective-permute-start(bf16[3,16,256]{2,1,0:T(8,128)(2,1)S(1)} %get-tuple-element.12), channel_id=1, source_target_pairs={{0,4},{1,5},{2,6},{3,7},{4,0},{5,1},{6,2},{7,3},{8,12},{9,13},{10,... | collective-permute-start | bytes 73736 | tf_op jit(solution)/shard_map/ppermute | solution.py:174
  5.8 4.1 %collective-permute-start.3 = (bf16[3,32,256]{2,1,0:T(8,128)(2,1)S(1)}, bf16[3,32,256]{2,1,0:T(8,128)(2,1)S(1)}, u32[]{:S(2)}, u32[]{:S(2)}) collective-permute-start(bf16[3,32,256]{2,1,0:T(8,128)(2,1)S(1)} %get-tuple-element.13), channel_id=1, source_target_pairs={{0,16},{8,24},{16,0},{24,8},{1,17},{9,25},{17,1},{25,9},{2,18},{10... | collective-permute-start | bytes 147464 | tf_op jit(solution)/shard_map/ppermute | solution.py:174
  7.6 4.2 %collective-permute-start.1 = (bf16[2,3,16,256]{3,2,1,0:T(8,128)(2,1)S(1)}, bf16[2,3,16,256]{3,2,1,0:T(8,128)(2,1)S(1)}, u32[]{:S(2)}, u32[]{:S(2)}) collective-permute-start(bf16[2,3,16,256]{3,2,1,0:T(8,128)(2,1)S(1)} %pad_maximum_fusion.12), channel_id=1, source_target_pairs={{0,2},{1,3},{2,0},{3,1},{4,6},{5,7},{6,4},{7,5},{8,10},{9,11},{10,... | collective-permute-start | bytes 147464 | tf_op jit(solution)/shard_map/ppermute | solution.py:174
  9.9 3.9 %collective-permute-start.4 = (bf16[2,3,32,256]{3,2,1,0:T(8,128)(2,1)S(1)}, bf16[2,3,32,256]{3,2,1,0:T(8,128)(2,1)S(1)}, u32[]{:S(2)}, u32[]{:S(2)}) collective-permute-start(bf16[2,3,32,256]{3,2,1,0:T(8,128)(2,1)S(1)} %pad_maximum_fusion.5), channel_id=1, source_target_pairs={{0,8},{8,0},{16,24},{24,16},{1,9},{9,1},{17,25},{25,17},{2,10},{10... | collective-permute-start | bytes 294920 | tf_op jit(solution)/shard_map/ppermute | solution.py:174
  11.8 4.7 %collective-permute-start.2 = (bf16[2,2,3,16,256]{4,3,2,0,1:T(8,128)(2,1)S(1)}, bf16[2,2,3,16,256]{4,3,2,0,1:T(8,128)(2,1)S(1)}, u32[]{:S(2)}, u32[]{:S(2)}) collective-permute-start(bf16[2,2,3,16,256]{4,3,2,0,1:T(8,128)(2,1)S(1)} %pad_maximum_fusion.4), channel_id=1, source_target_pairs={{0,1},{1,0},{2,3},{3,2},{4,5},{5,4},{6,7},{7,6},{8,9},{9,8},{10,11... | collective-permute-start | bytes 294920 | tf_op jit(solution)/shard_map/ppermute | solution.py:174
  16.6 32.6 %copy-start = (f32[128,256]{1,0:T(8,128)S(1)}, f32[128,256]{1,0:T(8,128)}, u32[]{:S(2)}) copy-start(f32[128,256]{1,0:T(8,128)} %refs_6_.1) | copy-start | bytes 393220
  16.6 32.6 %copy-start.1 = (f32[128,256]{1,0:T(8,128)S(1)}, f32[128,256]{1,0:T(8,128)}, u32[]{:S(2)}) copy-start(f32[128,256]{1,0:T(8,128)} %param.23) | copy-start | bytes 393220
  16.6 32.6 %copy-start.2 = (f32[128,256]{1,0:T(8,128)S(1)}, f32[128,256]{1,0:T(8,128)}, u32[]{:S(2)}) copy-start(f32[128,256]{1,0:T(8,128)} %param.22) | copy-start | bytes 393220
  26.8 1.4 %collective-permute-start.5 = (bf16[192,256]{1,0:T(8,128)(2,1)S(1)}, bf16[192,256]{1,0:T(8,128)(2,1)S(1)}, u32[]{:S(2)}, u32[]{:S(2)}) collective-permute-start(bf16[192,256]{1,0:T(8,128)(2,1)S(1)} %pad_maximum_fusion.6), channel_id=1, source_target_pairs={{0,8},{8,0},{16,24},{24,16},{1,9},{9,1},{17,25},{25,17},{2,10},{10... | collective-permute-start | bytes 294920 | tf_op jit(solution)/shard_map/ppermute | solution.py:174
  28.2 4.9 %collective-permute-start.8 = (bf16[64,256]{1,0:T(8,128)(2,1)S(1)}, bf16[64,256]{1,0:T(8,128)(2,1)S(1)}, u32[]{:S(2)}, u32[]{:S(2)}) collective-permute-start(bf16[64,256]{1,0:T(8,128)(2,1)S(1)} %add_convert_fusion.12), channel_id=1, source_target_pairs={{0,17},{1,16},{2,19},{3,18},{4,21},{5,20},{6,23},{7,22},{8,25},{9,... | collective-permute-start | bytes 98312 | tf_op jit(solution)/shard_map/ppermute | solution.py:198
  31.2 4.7 %collective-permute-start.6 = (bf16[192,256]{1,0:T(8,128)(2,1)S(1)}, bf16[192,256]{1,0:T(8,128)(2,1)S(1)}, u32[]{:S(2)}, u32[]{:S(2)}) collective-permute-start(bf16[192,256]{1,0:T(8,128)(2,1)S(1)} %get-tuple-element.42), channel_id=1, source_target_pairs={{0,1},{1,0},{2,3},{3,2},{4,5},{5,4},{6,7},{7,6},{8,9},{9,8},{10,11... | collective-permute-start | bytes 294920 | tf_op jit(solution)/shard_map/ppermute | solution.py:174
  31.8 4.6 %collective-permute-start.7 = (bf16[192,256]{1,0:T(8,128)(2,1)S(1)}, bf16[192,256]{1,0:T(8,128)(2,1)S(1)}, u32[]{:S(2)}, u32[]{:S(2)}) collective-permute-start(bf16[192,256]{1,0:T(8,128)(2,1)S(1)} %get-tuple-element.41), channel_id=1, source_target_pairs={{0,16},{8,24},{16,0},{24,8},{1,17},{9,25},{17,1},{25,9},{2,18},{10... | collective-permute-start | bytes 294920 | tf_op jit(solution)/shard_map/ppermute | solution.py:174
  36.5 4.7 %collective-permute-start.9 = (bf16[192,256]{1,0:T(8,128)(2,1)S(1)}, bf16[192,256]{1,0:T(8,128)(2,1)S(1)}, u32[]{:S(2)}, u32[]{:S(2)}) collective-permute-start(bf16[192,256]{1,0:T(8,128)(2,1)S(1)} %pad_maximum_fusion.7), channel_id=1, source_target_pairs={{0,2},{1,3},{2,0},{3,1},{4,6},{5,7},{6,4},{7,5},{8,10},{9,11},{10,... | collective-permute-start | bytes 294920 | tf_op jit(solution)/shard_map/ppermute | solution.py:174
  41.2 6.6 %collective-permute-start.10 = (bf16[192,256]{1,0:T(8,128)(2,1)S(1)}, bf16[192,256]{1,0:T(8,128)(2,1)S(1)}, u32[]{:S(2)}, u32[]{:S(2)}) collective-permute-start(bf16[192,256]{1,0:T(8,128)(2,1)S(1)} %pad_maximum_fusion.8), channel_id=1, source_target_pairs={{0,4},{1,5},{2,6},{3,7},{4,0},{5,1},{6,2},{7,3},{8,12},{9,13},{10,... | collective-permute-start | bytes 294920 | tf_op jit(solution)/shard_map/ppermute | solution.py:174
  47.9 1.3 %collective-permute-start.11 = (bf16[64,256]{1,0:T(8,128)(2,1)S(1)}, bf16[64,256]{1,0:T(8,128)(2,1)S(1)}, u32[]{:S(2)}, u32[]{:S(2)}) collective-permute-start(bf16[64,256]{1,0:T(8,128)(2,1)S(1)} %add_convert_fusion.9), channel_id=1, source_target_pairs={{0,8},{8,0},{16,24},{24,16},{1,9},{9,1},{17,25},{25,17},{2,10},{10... | collective-permute-start | bytes 98312 | tf_op jit(solution)/shard_map/ppermute | solution.py:174
  48.0 25.5 %copy-start.3 = (f32[32,256]{1,0:T(8,128)S(1)}, f32[32,256]{1,0:T(8,128)}, u32[]{:S(2)}) copy-start(f32[32,256]{1,0:T(8,128)} %refs_3_.1) | copy-start | bytes 98308
  48.0 25.5 %copy-start.4 = (f32[32,256]{1,0:T(8,128)S(1)}, f32[32,256]{1,0:T(8,128)}, u32[]{:S(2)}) copy-start(f32[32,256]{1,0:T(8,128)} %refs_4_.1) | copy-start | bytes 98308
  48.0 25.5 %copy-start.5 = (f32[32,256]{1,0:T(8,128)S(1)}, f32[32,256]{1,0:T(8,128)}, u32[]{:S(2)}) copy-start(f32[32,256]{1,0:T(8,128)} %refs_5_.1) | copy-start | bytes 98308
  48.0 28.2 %copy-start.6 = (f32[16,256]{1,0:T(8,128)S(1)}, f32[16,256]{1,0:T(8,128)}, u32[]{:S(2)}) copy-start(f32[16,256]{1,0:T(8,128)} %refs_0_.1) | copy-start | bytes 49156
  48.0 28.2 %copy-start.7 = (f32[16,256]{1,0:T(8,128)S(1)}, f32[16,256]{1,0:T(8,128)}, u32[]{:S(2)}) copy-start(f32[16,256]{1,0:T(8,128)} %refs_1_.1) | copy-start | bytes 49156
  48.0 28.2 %copy-start.8 = (f32[16,256]{1,0:T(8,128)S(1)}, f32[16,256]{1,0:T(8,128)}, u32[]{:S(2)}) copy-start(f32[16,256]{1,0:T(8,128)} %refs_2_.1) | copy-start | bytes 49156
  59.7 1.3 %collective-permute-start.12 = (bf16[128,256]{1,0:T(8,128)(2,1)S(1)}, bf16[128,256]{1,0:T(8,128)(2,1)S(1)}, u32[]{:S(2)}, u32[]{:S(2)}) collective-permute-start(bf16[128,256]{1,0:T(8,128)(2,1)S(1)} %pad_maximum_fusion.10), channel_id=1, source_target_pairs={{0,8},{8,0},{16,24},{24,16},{1,9},{9,1},{17,25},{25,17},{2,10},{10... | collective-permute-start | bytes 196616 | tf_op jit(solution)/shard_map/ppermute | solution.py:174
  61.0 5.8 %collective-permute-start.15 = (bf16[64,256]{1,0:T(8,128)(2,1)S(1)}, bf16[64,256]{1,0:T(8,128)(2,1)S(1)}, u32[]{:S(2)}, u32[]{:S(2)}) collective-permute-start(bf16[64,256]{1,0:T(8,128)(2,1)S(1)} %add_convert_fusion.8), channel_id=1, source_target_pairs={{0,17},{1,16},{2,19},{3,18},{4,21},{5,20},{6,23},{7,22},{8,25},{9,... | collective-permute-start | bytes 98312 | tf_op jit(solution)/shard_map/ppermute | solution.py:198
  62.5 4.3 %collective-permute-start.13 = (bf16[128,256]{1,0:T(8,128)(2,1)S(1)}, bf16[128,256]{1,0:T(8,128)(2,1)S(1)}, u32[]{:S(2)}, u32[]{:S(2)}) collective-permute-start(bf16[128,256]{1,0:T(8,128)(2,1)S(1)} %pad_maximum_fusion.11), channel_id=1, source_target_pairs={{0,1},{1,0},{2,3},{3,2},{4,5},{5,4},{6,7},{7,6},{8,9},{9,8},{10,11... | collective-permute-start | bytes 196616 | tf_op jit(solution)/shard_map/ppermute | solution.py:174
  62.7 4.2 %collective-permute-start.14 = (bf16[96,256]{1,0:T(8,128)(2,1)S(1)}, bf16[96,256]{1,0:T(8,128)(2,1)S(1)}, u32[]{:S(2)}, u32[]{:S(2)}) collective-permute-start(bf16[96,256]{1,0:T(8,128)(2,1)S(1)} %pad_maximum_fusion.13), channel_id=1, source_target_pairs={{0,16},{8,24},{16,0},{24,8},{1,17},{9,25},{17,1},{25,9},{2,18},{10... | collective-permute-start | bytes 147464 | tf_op jit(solution)/shard_map/ppermute | solution.py:174
  66.9 4.2 %collective-permute-start.16 = (bf16[96,256]{1,0:T(8,128)(2,1)S(1)}, bf16[96,256]{1,0:T(8,128)(2,1)S(1)}, u32[]{:S(2)}, u32[]{:S(2)}) collective-permute-start(bf16[96,256]{1,0:T(8,128)(2,1)S(1)} %pad_maximum_fusion.14), channel_id=1, source_target_pairs={{0,2},{1,3},{2,0},{3,1},{4,6},{5,7},{6,4},{7,5},{8,10},{9,11},{10,... | collective-permute-start | bytes 147464 | tf_op jit(solution)/shard_map/ppermute | solution.py:174
  71.1 5.0 %collective-permute-start.17 = (bf16[80,256]{1,0:T(8,128)(2,1)S(1)}, bf16[80,256]{1,0:T(8,128)(2,1)S(1)}, u32[]{:S(2)}, u32[]{:S(2)}) collective-permute-start(bf16[80,256]{1,0:T(8,128)(2,1)S(1)} %pad_maximum_fusion.15), channel_id=1, source_target_pairs={{0,4},{1,5},{2,6},{3,7},{4,0},{5,1},{6,2},{7,3},{8,12},{9,13},{10,... | collective-permute-start | bytes 122888 | tf_op jit(solution)/shard_map/ppermute | solution.py:174
  76.1 1.3 %collective-permute-start.18 = (bf16[64,256]{1,0:T(8,128)(2,1)S(1)}, bf16[64,256]{1,0:T(8,128)(2,1)S(1)}, u32[]{:S(2)}, u32[]{:S(2)}) collective-permute-start(bf16[64,256]{1,0:T(8,128)(2,1)S(1)} %add_convert_fusion.5), channel_id=1, source_target_pairs={{0,8},{8,0},{16,24},{24,16},{1,9},{9,1},{17,25},{25,17},{2,10},{10... | collective-permute-start | bytes 98312 | tf_op jit(solution)/shard_map/ppermute | solution.py:174

commit v4 on v3

--- a/solution.py
+++ b/solution.py
@@ -34,23 +34,22 @@
 
 def tile_gradients(
     table_ref, obs_ref, bucket_ref, camp_ref, hour_ref, delay_ref,
-    ga_ref, gb_ref, gc_ref, gb_sum, gc_sum, parts, arrived,
+    ga_ref, gb_ref, gc_ref, gb_sum, gc_sum, cuts, arrived,
 ):
-    total, cols, delays = obs_ref.shape
+    cols, delays = obs_ref.shape[1:]
     rank = hour_ref.shape[1]
-    rows = total // parts
-    sub = math.gcd(rows, 8)
+    sub = math.gcd(*cuts, 8)
     flat = sub * cols
     gb_sum[...] = jnp.zeros_like(gb_sum)
     gc_sum[...] = jnp.zeros_like(gc_sum)
     hour16 = hour_ref[...]
     hour = hour16.astype(F32)
     delay = delay_ref[...]
-    for part in range(parts):
+    for part in range(len(cuts) - 1):
         arrived(part)
         table = jnp.broadcast_to(table_ref[:1], (flat, delays))
         gb_part, gc_part = gb_sum[...], gc_sum[...]
-        for start in range(part * rows, (part + 1) * rows, sub):
+        for start in range(cuts[part], cuts[part + 1], sub):
             camp = camp_ref[start:start + sub]
             pair = (camp[:, None, :] * hour16[None, :, :]).reshape(flat, rank)
             model = lax.dot_general(pair, delay, (((1,), (1,)), ((), ())), preferred_element_type=F32)
@@ -69,6 +68,14 @@
 
 
 AHEAD = 3
+SHARES = (1, 1, 2, 4)
+
+
+def cuts_of(rows):
+    unit = rows // sum(SHARES)
+    if unit * sum(SHARES) != rows or unit % 8:
+        return (0, rows)
+    return tuple(unit * sum(SHARES[:n]) for n in range(len(SHARES) + 1))
 
 
 def grads_kernel(
@@ -76,11 +83,11 @@
     ga_ref, gb_ref, gc_ref,
     gb_sum, gc_sum, table_ref, obs_ref, bucket_ref, prop_ref, prop_sem, sems,
 ):
-    parts = sems.shape[1]
-    rows = obs_ref.shape[0] // parts
+    cuts = cuts_of(obs_ref.shape[0])
+    parts = len(cuts) - 1
 
     def fetches(part):
-        at = pl.ds(part * rows, rows)
+        at = pl.ds(cuts[part], cuts[part + 1] - cuts[part])
         return (
             pltpu.make_async_copy(obs_hbm.at[at], obs_ref.at[at], sems.at[0, part]),
             pltpu.make_async_copy(bucket_hbm.at[at], bucket_ref.at[at], sems.at[1, part]),
@@ -104,14 +111,14 @@
     fill_table(table_ref, prop_ref)
     tile_gradients(
         table_ref, obs_ref, bucket_ref, camp_ref, hour_ref, delay_ref,
-        ga_ref, gb_ref, gc_ref, gb_sum, gc_sum, parts, arrived,
+        ga_ref, gb_ref, gc_ref, gb_sum, gc_sum, cuts, arrived,
     )
 
 
 def gradients(propensity, observed, bucket, camp_block, hour_block, delay_block):
     tile_rows, tile_cols, delay_count = observed.shape
     rank = camp_block.shape[1]
-    parts = tile_rows // math.gcd(tile_rows, 16)
+    parts = len(cuts_of(tile_rows)) - 1
     vmem = pl.BlockSpec(memory_space=pltpu.VMEM)
     hbm = pl.BlockSpec(memory_space=pltpu.HBM)
     large = [pltpu.with_memory_space_constraint(x, pltpu.HBM) for x in (propensity, observed, bucket)]

time: 78.4 us -> 77.8 us (level)
  no operation moved by 1% of the time
where the time goes in v4:
time: 77.8 us; the launch traced here: 77.6 us
  waiting for transfers between devices  27.6 us (35%)
  starting transfers between devices  24.8 us (32%)
  Pallas kernels  20.8 us (27%)
  other arithmetic  3.13 us (4%)
  between operations  1.17 us (2%)
    ppermute x17, waiting for transfers between devices, swap(): return lax.ppermute(block, axis, [(i, i ^ bit) for i in range(size)])  26.4 us
    ppermute x17, starting transfers between devices, swap(): return lax.ppermute(block, axis, [(i, i ^ bit) for i in range(size)])  20.3 us
    pallas_call x2, Pallas kernels, gradients(): pl.pallas_call(grads_kernel, in_specs=[hbm] * 3 + [vmem] * 3, out_specs=[...  19.7 us
    ppermute x2, starting transfers between devices, swap_both(): lax.ppermute(block, ('camp', 'hour'), [(i, i ^ camp_bit * hours + hour_bi...  4.5 us
    sub x3, other arithmetic, adam_update(): factor = factor - learn_rate * moment / (jnp.sqrt(second) + adam_eps)  2.17 us
  transfers between devices with their start and end apart: 19, of which 16 were waited for; matrix products, arithmetic and copies ran while one was open for 2% of the time, Pallas kernels for 0%

profile of v4, /device:TPU:0, one launch (start us, length us, event | category | flops | bytes accessed | tf_op | source)
XLA Modules:
  0.0 77.6 jit_solution(18222141021037400052)
XLA Ops:
  0.6 1.0 %pack.1 = (bf16[3,16,256]{2,1,0:T(8,128)(2,1)S(1)}, bf16[3,32,256]{2,1,0:T(8,128)(2,1)S(1)}, bf16[128,256]{1,0:T(8,128)(2,1)S(1)}) custom-call(f32[16,256]{1,0:T(8,128)} %refs_0_.1, f32[16,256]{1,0:T(8,128)} %refs_1_.1, f32[16,256]{1,0:T(8,128)} %refs_2_.1, f32[32,256]{1,0:T(8,128)} %refs_3_.1, f32[32,256]{1,0:T(8,128)} %refs_4_.1, f32[32,256]{1,0:T(8,128)} %refs_5_.1, ...), custom_call_target="tpu_custom_call" | custom-call | tf_op jit(solution)/shard_map/pack/pallas_call | solution.py:165
  1.7 4.1 %collective-permute-start = (bf16[3,16,256]{2,1,0:T(8,128)(2,1)S(1)}, bf16[3,16,256]{2,1,0:T(8,128)(2,1)S(1)}, u32[]{:S(2)}, u32[]{:S(2)}) collective-permute-start(bf16[3,16,256]{2,1,0:T(8,128)(2,1)S(1)} %get-tuple-element.12), channel_id=1, source_target_pairs={{0,4},{1,5},{2,6},{3,7},{4,0},{5,1},{6,2},{7,3},{8,12},{9,13},{10,... | collective-permute-start | bytes 73736 | tf_op jit(solution)/shard_map/ppermute | solution.py:181
  5.8 1.5 %collective-permute-start.3 = (bf16[3,32,256]{2,1,0:T(8,128)(2,1)S(1)}, bf16[3,32,256]{2,1,0:T(8,128)(2,1)S(1)}, u32[]{:S(2)}, u32[]{:S(2)}) collective-permute-start(bf16[3,32,256]{2,1,0:T(8,128)(2,1)S(1)} %get-tuple-element.13), channel_id=1, source_target_pairs={{0,16},{8,24},{16,0},{24,8},{1,17},{9,25},{17,1},{25,9},{2,18},{10... | collective-permute-start | bytes 147464 | tf_op jit(solution)/shard_map/ppermute | solution.py:181
  7.6 2.0 %collective-permute-start.1 = (bf16[2,3,16,256]{3,2,1,0:T(8,128)(2,1)S(1)}, bf16[2,3,16,256]{3,2,1,0:T(8,128)(2,1)S(1)}, u32[]{:S(2)}, u32[]{:S(2)}) collective-permute-start(bf16[2,3,16,256]{3,2,1,0:T(8,128)(2,1)S(1)} %pad_maximum_fusion.12), channel_id=1, source_target_pairs={{0,2},{1,3},{2,0},{3,1},{4,6},{5,7},{6,4},{7,5},{8,10},{9,11},{10,... | collective-permute-start | bytes 147464 | tf_op jit(solution)/shard_map/ppermute | solution.py:181
  10.0 1.8 %collective-permute-done.1 = bf16[2,3,16,256]{3,2,1,0:T(8,128)(2,1)S(1)} collective-permute-done((bf16[2,3,16,256]{3,2,1,0:T(8,128)(2,1)S(1)}, bf16[2,3,16,256]{3,2,1,0:T(8,128)(2,1)S(1)}, u32[]{:S(2)}, u32[]{:S(2)}) %collective-permute-start.1) | collective-permute-done | bytes 49184 | tf_op jit(solution)/shard_map/ppermute | solution.py:181
  11.8 2.0 %collective-permute-start.2 = (bf16[2,2,3,16,256]{4,3,2,0,1:T(8,128)(2,1)S(1)}, bf16[2,2,3,16,256]{4,3,2,0,1:T(8,128)(2,1)S(1)}, u32[]{:S(2)}, u32[]{:S(2)}) collective-permute-start(bf16[2,2,3,16,256]{4,3,2,0,1:T(8,128)(2,1)S(1)} %pad_maximum_fusion.4), channel_id=1, source_target_pairs={{0,1},{1,0},{2,3},{3,2},{4,5},{5,4},{6,7},{7,6},{8,9},{9,8},{10,11... | collective-permute-start | bytes 294920 | tf_op jit(solution)/shard_map/ppermute | solution.py:181
  13.9 2.6 %collective-permute-done.2 = bf16[2,2,3,16,256]{4,3,2,0,1:T(8,128)(2,1)S(1)} collective-permute-done((bf16[2,2,3,16,256]{4,3,2,0,1:T(8,128)(2,1)S(1)}, bf16[2,2,3,16,256]{4,3,2,0,1:T(8,128)(2,1)S(1)}, u32[]{:S(2)}, u32[]{:S(2)}) %collective-permute-start.2) | collective-permute-done | bytes 98336 | tf_op jit(solution)/shard_map/ppermute | solution.py:181
  16.6 9.8 %gradients.2 = (f32[128,256]{1,0:T(8,128)S(1)}, bf16[128,256]{1,0:T(8,128)(2,1)S(1)}, bf16[128,256]{1,0:T(8,128)(2,1)S(1)}) custom-call(f32[8]{0:T(128)} %prop_hbm.3, bf16[128,128,128]{2,1,0:T(8,128)(2,1)} %obs_hbm.3, s32[128,128,128]{2,1,0:T(8,128)} %bucket_hbm.3, bf16[128,256]{1,0:T(8,128)(2,1)S(1)} %bitcast.109, bf16[128,256]{1,0:T(8,128)(2,1)S(1)} %bitcast.108, ...), custom_call_target="tpu_custom_call" | custom-call | flops 3221225472 | bytes 12582912 | tf_op jit(solution)/shard_map/gradients/pallas_call | solution.py:125
  26.6 1.3 %collective-permute-done.5 = bf16[192,256]{1,0:T(8,128)(2,1)S(1)} collective-permute-done((bf16[192,256]{1,0:T(8,128)(2,1)S(1)}, bf16[192,256]{1,0:T(8,128)(2,1)S(1)}, u32[]{:S(2)}, u32[]{:S(2)}) %collective-permute-start.5) | collective-permute-done | bytes 98336 | tf_op jit(solution)/shard_map/ppermute | solution.py:181
  27.9 3.0 %collective-permute-start.8 = (bf16[64,256]{1,0:T(8,128)(2,1)S(1)}, bf16[64,256]{1,0:T(8,128)(2,1)S(1)}, u32[]{:S(2)}, u32[]{:S(2)}) collective-permute-start(bf16[64,256]{1,0:T(8,128)(2,1)S(1)} %add_convert_fusion.12), channel_id=1, source_target_pairs={{0,17},{1,16},{2,19},{3,18},{4,21},{5,20},{6,23},{7,22},{8,25},{9,... | collective-permute-start | bytes 98312 | tf_op jit(solution)/shard_map/ppermute | solution.py:205
  30.9 0.6 collective-permute-start.6
  31.5 1.2 %collective-permute-done.8 = bf16[64,256]{1,0:T(8,128)(2,1)S(1)} collective-permute-done((bf16[64,256]{1,0:T(8,128)(2,1)S(1)}, bf16[64,256]{1,0:T(8,128)(2,1)S(1)}, u32[]{:S(2)}, u32[]{:S(2)}) %collective-permute-start.8) | collective-permute-done | bytes 32800 | tf_op jit(solution)/shard_map/ppermute | solution.py:205
  32.7 2.8 %collective-permute-done.6 = bf16[192,256]{1,0:T(8,128)(2,1)S(1)} collective-permute-done((bf16[192,256]{1,0:T(8,128)(2,1)S(1)}, bf16[192,256]{1,0:T(8,128)(2,1)S(1)}, u32[]{:S(2)}, u32[]{:S(2)}) %collective-permute-start.6) | collective-permute-done | bytes 98336 | tf_op jit(solution)/shard_map/ppermute | solution.py:181
  35.5 0.5 collective-permute-done.7
  36.1 1.5 %collective-permute-start.9 = (bf16[192,256]{1,0:T(8,128)(2,1)S(1)}, bf16[192,256]{1,0:T(8,128)(2,1)S(1)}, u32[]{:S(2)}, u32[]{:S(2)}) collective-permute-start(bf16[192,256]{1,0:T(8,128)(2,1)S(1)} %pad_maximum_fusion.7), channel_id=1, source_target_pairs={{0,2},{1,3},{2,0},{3,1},{4,6},{5,7},{6,4},{7,5},{8,10},{9,11},{10,... | collective-permute-start | bytes 294920 | tf_op jit(solution)/shard_map/ppermute | solution.py:181
  37.7 3.2 %collective-permute-done.9 = bf16[192,256]{1,0:T(8,128)(2,1)S(1)} collective-permute-done((bf16[192,256]{1,0:T(8,128)(2,1)S(1)}, bf16[192,256]{1,0:T(8,128)(2,1)S(1)}, u32[]{:S(2)}, u32[]{:S(2)}) %collective-permute-start.9) | collective-permute-done | bytes 98336 | tf_op jit(solution)/shard_map/ppermute | solution.py:181
  40.9 2.5 %collective-permute-start.10 = (bf16[192,256]{1,0:T(8,128)(2,1)S(1)}, bf16[192,256]{1,0:T(8,128)(2,1)S(1)}, u32[]{:S(2)}, u32[]{:S(2)}) collective-permute-start(bf16[192,256]{1,0:T(8,128)(2,1)S(1)} %pad_maximum_fusion.8), channel_id=1, source_target_pairs={{0,4},{1,5},{2,6},{3,7},{4,0},{5,1},{6,2},{7,3},{8,12},{9,13},{10,... | collective-permute-start | bytes 294920 | tf_op jit(solution)/shard_map/ppermute | solution.py:181
  43.5 4.1 %collective-permute-done.10 = bf16[192,256]{1,0:T(8,128)(2,1)S(1)} collective-permute-done((bf16[192,256]{1,0:T(8,128)(2,1)S(1)}, bf16[192,256]{1,0:T(8,128)(2,1)S(1)}, u32[]{:S(2)}, u32[]{:S(2)}) %collective-permute-start.10) | collective-permute-done | bytes 98336 | tf_op jit(solution)/shard_map/ppermute | solution.py:181
  47.9 0.9 %collective-permute-done.11 = bf16[64,256]{1,0:T(8,128)(2,1)S(1)} collective-permute-done((bf16[64,256]{1,0:T(8,128)(2,1)S(1)}, bf16[64,256]{1,0:T(8,128)(2,1)S(1)}, u32[]{:S(2)}, u32[]{:S(2)}) %collective-permute-start.11) | collective-permute-done | bytes 32800 | tf_op jit(solution)/shard_map/ppermute | solution.py:181
  49.0 9.9 %gradients.3 = (f32[128,256]{1,0:T(8,128)S(1)}, bf16[128,256]{1,0:T(8,128)(2,1)S(1)}, bf16[128,256]{1,0:T(8,128)(2,1)S(1)}) custom-call(f32[8]{0:T(128)} %prop_hbm.3, bf16[128,128,128]{2,1,0:T(8,128)(2,1)} %obs_hbm.3, s32[128,128,128]{2,1,0:T(8,128)} %bucket_hbm.3, bf16[128,256]{1,0:T(8,128)(2,1)S(1)} %get-tuple-element.43.camp_ref, ...), custom_call_target="tpu_custom_call" | custom-call | flops 3221225472 | bytes 12582912 | tf_op jit(solution)/shard_map/gradients/pallas_call | solution.py:125
  59.2 1.1 %collective-permute-done.12 = bf16[128,256]{1,0:T(8,128)(2,1)S(1)} collective-permute-done((bf16[128,256]{1,0:T(8,128)(2,1)S(1)}, bf16[128,256]{1,0:T(8,128)(2,1)S(1)}, u32[]{:S(2)}, u32[]{:S(2)}) %collective-permute-start.12) | collective-permute-done | bytes 65568 | tf_op jit(solution)/shard_map/ppermute | solution.py:181
  60.3 1.5 %collective-permute-start.15 = (bf16[64,256]{1,0:T(8,128)(2,1)S(1)}, bf16[64,256]{1,0:T(8,128)(2,1)S(1)}, u32[]{:S(2)}, u32[]{:S(2)}) collective-permute-start(bf16[64,256]{1,0:T(8,128)(2,1)S(1)} %add_convert_fusion.8), channel_id=1, source_target_pairs={{0,17},{1,16},{2,19},{3,18},{4,21},{5,20},{6,23},{7,22},{8,25},{9,... | collective-permute-start | bytes 98312 | tf_op jit(solution)/shard_map/ppermute | solution.py:205
  62.0 2.0 %collective-permute-start.14 = (bf16[96,256]{1,0:T(8,128)(2,1)S(1)}, bf16[96,256]{1,0:T(8,128)(2,1)S(1)}, u32[]{:S(2)}, u32[]{:S(2)}) collective-permute-start(bf16[96,256]{1,0:T(8,128)(2,1)S(1)} %pad_maximum_fusion.13), channel_id=1, source_target_pairs={{0,16},{8,24},{16,0},{24,8},{1,17},{9,25},{17,1},{25,9},{2,18},{10... | collective-permute-start | bytes 147464 | tf_op jit(solution)/shard_map/ppermute | solution.py:181
  64.0 2.1 %collective-permute-done.13 = bf16[128,256]{1,0:T(8,128)(2,1)S(1)} collective-permute-done((bf16[128,256]{1,0:T(8,128)(2,1)S(1)}, bf16[128,256]{1,0:T(8,128)(2,1)S(1)}, u32[]{:S(2)}, u32[]{:S(2)}) %collective-permute-start.13) | collective-permute-done | bytes 65568 | tf_op jit(solution)/shard_map/ppermute | solution.py:181
  66.2 1.0 %collective-permute-start.16 = (bf16[96,256]{1,0:T(8,128)(2,1)S(1)}, bf16[96,256]{1,0:T(8,128)(2,1)S(1)}, u32[]{:S(2)}, u32[]{:S(2)}) collective-permute-start(bf16[96,256]{1,0:T(8,128)(2,1)S(1)} %pad_maximum_fusion.14), channel_id=1, source_target_pairs={{0,2},{1,3},{2,0},{3,1},{4,6},{5,7},{6,4},{7,5},{8,10},{9,11},{10,... | collective-permute-start | bytes 147464 | tf_op jit(solution)/shard_map/ppermute | solution.py:181
  67.3 3.1 %collective-permute-done.16 = bf16[96,256]{1,0:T(8,128)(2,1)S(1)} collective-permute-done((bf16[96,256]{1,0:T(8,128)(2,1)S(1)}, bf16[96,256]{1,0:T(8,128)(2,1)S(1)}, u32[]{:S(2)}, u32[]{:S(2)}) %collective-permute-start.16) | collective-permute-done | bytes 49184 | tf_op jit(solution)/shard_map/ppermute | solution.py:181
  70.4 2.4 %collective-permute-start.17 = (bf16[80,256]{1,0:T(8,128)(2,1)S(1)}, bf16[80,256]{1,0:T(8,128)(2,1)S(1)}, u32[]{:S(2)}, u32[]{:S(2)}) collective-permute-start(bf16[80,256]{1,0:T(8,128)(2,1)S(1)} %pad_maximum_fusion.15), channel_id=1, source_target_pairs={{0,4},{1,5},{2,6},{3,7},{4,0},{5,1},{6,2},{7,3},{8,12},{9,13},{10,... | collective-permute-start | bytes 122888 | tf_op jit(solution)/shard_map/ppermute | solution.py:181
  72.8 0.7 fusion.28
  73.5 1.9 %collective-permute-done.17 = bf16[80,256]{1,0:T(8,128)(2,1)S(1)} collective-permute-done((bf16[80,256]{1,0:T(8,128)(2,1)S(1)}, bf16[80,256]{1,0:T(8,128)(2,1)S(1)}, u32[]{:S(2)}, u32[]{:S(2)}) %collective-permute-start.17) | collective-permute-done | bytes 40992 | tf_op jit(solution)/shard_map/ppermute | solution.py:181
  75.6 0.6 fusion.38
  76.2 0.5 collective-permute-done.18
  76.7 0.8 %fusion.6 = f32[128,256]{1,0:T(8,128)} fusion(f32[128,256]{1,0:T(8,128)S(1)} %copy-done.2, bf16[64,256]{1,0:T(8,128)(2,1)S(1)} %get-tuple-element.34, bf16[64,256]{1,0:T(8,128)(2,1)S(1)} %get-tuple-element.33, f32[128,256]{1,0:T(8,128)S(1)} %copy-done.1, bf16[64,256]{1,0:T(8,128)(2,1)S(1)} %get-tuple-element.38, bf16[64,256]{1,0:T(8,128)(2,1)S(1)} %get-tuple-element.37, ...), kind=kLoop, calls=%fused_computation.14 | loop fusion | flops 1048576 | bytes 655360 | tf_op jit(solution)/shard_map/sub | solution.py:23
  (93 shorter events, 2.4 us)
Async XLA Ops:
  1.7 5.9 %collective-permute-start = (bf16[3,16,256]{2,1,0:T(8,128)(2,1)S(1)}, bf16[3,16,256]{2,1,0:T(8,128)(2,1)S(1)}, u32[]{:S(2)}, u32[]{:S(2)}) collective-permute-start(bf16[3,16,256]{2,1,0:T(8,128)(2,1)S(1)} %get-tuple-element.12), channel_id=1, source_target_pairs={{0,4},{1,5},{2,6},{3,7},{4,0},{5,1},{6,2},{7,3},{8,12},{9,13},{10,... | collective-permute-start | bytes 73736 | tf_op jit(solution)/shard_map/ppermute | solution.py:181
  5.8 4.1 %collective-permute-start.3 = (bf16[3,32,256]{2,1,0:T(8,128)(2,1)S(1)}, bf16[3,32,256]{2,1,0:T(8,128)(2,1)S(1)}, u32[]{:S(2)}, u32[]{:S(2)}) collective-permute-start(bf16[3,32,256]{2,1,0:T(8,128)(2,1)S(1)} %get-tuple-element.13), channel_id=1, source_target_pairs={{0,16},{8,24},{16,0},{24,8},{1,17},{9,25},{17,1},{25,9},{2,18},{10... | collective-permute-start | bytes 147464 | tf_op jit(solution)/shard_map/ppermute | solution.py:181
  7.6 4.2 %collective-permute-start.1 = (bf16[2,3,16,256]{3,2,1,0:T(8,128)(2,1)S(1)}, bf16[2,3,16,256]{3,2,1,0:T(8,128)(2,1)S(1)}, u32[]{:S(2)}, u32[]{:S(2)}) collective-permute-start(bf16[2,3,16,256]{3,2,1,0:T(8,128)(2,1)S(1)} %pad_maximum_fusion.12), channel_id=1, source_target_pairs={{0,2},{1,3},{2,0},{3,1},{4,6},{5,7},{6,4},{7,5},{8,10},{9,11},{10,... | collective-permute-start | bytes 147464 | tf_op jit(solution)/shard_map/ppermute | solution.py:181
  9.9 3.9 %collective-permute-start.4 = (bf16[2,3,32,256]{3,2,1,0:T(8,128)(2,1)S(1)}, bf16[2,3,32,256]{3,2,1,0:T(8,128)(2,1)S(1)}, u32[]{:S(2)}, u32[]{:S(2)}) collective-permute-start(bf16[2,3,32,256]{3,2,1,0:T(8,128)(2,1)S(1)} %pad_maximum_fusion.5), channel_id=1, source_target_pairs={{0,8},{8,0},{16,24},{24,16},{1,9},{9,1},{17,25},{25,17},{2,10},{10... | collective-permute-start | bytes 294920 | tf_op jit(solution)/shard_map/ppermute | solution.py:181
  11.8 4.7 %collective-permute-start.2 = (bf16[2,2,3,16,256]{4,3,2,0,1:T(8,128)(2,1)S(1)}, bf16[2,2,3,16,256]{4,3,2,0,1:T(8,128)(2,1)S(1)}, u32[]{:S(2)}, u32[]{:S(2)}) collective-permute-start(bf16[2,2,3,16,256]{4,3,2,0,1:T(8,128)(2,1)S(1)} %pad_maximum_fusion.4), channel_id=1, source_target_pairs={{0,1},{1,0},{2,3},{3,2},{4,5},{5,4},{6,7},{7,6},{8,9},{9,8},{10,11... | collective-permute-start | bytes 294920 | tf_op jit(solution)/shard_map/ppermute | solution.py:181
  16.6 32.2 %copy-start = (f32[128,256]{1,0:T(8,128)S(1)}, f32[128,256]{1,0:T(8,128)}, u32[]{:S(2)}) copy-start(f32[128,256]{1,0:T(8,128)} %refs_6_.1) | copy-start | bytes 393220
  16.6 32.2 %copy-start.1 = (f32[128,256]{1,0:T(8,128)S(1)}, f32[128,256]{1,0:T(8,128)}, u32[]{:S(2)}) copy-start(f32[128,256]{1,0:T(8,128)} %param.23) | copy-start | bytes 393220
  16.6 32.2 %copy-start.2 = (f32[128,256]{1,0:T(8,128)S(1)}, f32[128,256]{1,0:T(8,128)}, u32[]{:S(2)}) copy-start(f32[128,256]{1,0:T(8,128)} %param.22) | copy-start | bytes 393220
  26.5 1.4 %collective-permute-start.5 = (bf16[192,256]{1,0:T(8,128)(2,1)S(1)}, bf16[192,256]{1,0:T(8,128)(2,1)S(1)}, u32[]{:S(2)}, u32[]{:S(2)}) collective-permute-start(bf16[192,256]{1,0:T(8,128)(2,1)S(1)} %pad_maximum_fusion.6), channel_id=1, source_target_pairs={{0,8},{8,0},{16,24},{24,16},{1,9},{9,1},{17,25},{25,17},{2,10},{10... | collective-permute-start | bytes 294920 | tf_op jit(solution)/shard_map/ppermute | solution.py:181
  27.9 4.9 %collective-permute-start.8 = (bf16[64,256]{1,0:T(8,128)(2,1)S(1)}, bf16[64,256]{1,0:T(8,128)(2,1)S(1)}, u32[]{:S(2)}, u32[]{:S(2)}) collective-permute-start(bf16[64,256]{1,0:T(8,128)(2,1)S(1)} %add_convert_fusion.12), channel_id=1, source_target_pairs={{0,17},{1,16},{2,19},{3,18},{4,21},{5,20},{6,23},{7,22},{8,25},{9,... | collective-permute-start | bytes 98312 | tf_op jit(solution)/shard_map/ppermute | solution.py:205
  30.9 4.7 %collective-permute-start.6 = (bf16[192,256]{1,0:T(8,128)(2,1)S(1)}, bf16[192,256]{1,0:T(8,128)(2,1)S(1)}, u32[]{:S(2)}, u32[]{:S(2)}) collective-permute-start(bf16[192,256]{1,0:T(8,128)(2,1)S(1)} %get-tuple-element.42), channel_id=1, source_target_pairs={{0,1},{1,0},{2,3},{3,2},{4,5},{5,4},{6,7},{7,6},{8,9},{9,8},{10,11... | collective-permute-start | bytes 294920 | tf_op jit(solution)/shard_map/ppermute | solution.py:181
  31.5 4.6 %collective-permute-start.7 = (bf16[192,256]{1,0:T(8,128)(2,1)S(1)}, bf16[192,256]{1,0:T(8,128)(2,1)S(1)}, u32[]{:S(2)}, u32[]{:S(2)}) collective-permute-start(bf16[192,256]{1,0:T(8,128)(2,1)S(1)} %get-tuple-element.41), channel_id=1, source_target_pairs={{0,16},{8,24},{16,0},{24,8},{1,17},{9,25},{17,1},{25,9},{2,18},{10... | collective-permute-start | bytes 294920 | tf_op jit(solution)/shard_map/ppermute | solution.py:181
  36.1 4.7 %collective-permute-start.9 = (bf16[192,256]{1,0:T(8,128)(2,1)S(1)}, bf16[192,256]{1,0:T(8,128)(2,1)S(1)}, u32[]{:S(2)}, u32[]{:S(2)}) collective-permute-start(bf16[192,256]{1,0:T(8,128)(2,1)S(1)} %pad_maximum_fusion.7), channel_id=1, source_target_pairs={{0,2},{1,3},{2,0},{3,1},{4,6},{5,7},{6,4},{7,5},{8,10},{9,11},{10,... | collective-permute-start | bytes 294920 | tf_op jit(solution)/shard_map/ppermute | solution.py:181
  40.9 6.6 %collective-permute-start.10 = (bf16[192,256]{1,0:T(8,128)(2,1)S(1)}, bf16[192,256]{1,0:T(8,128)(2,1)S(1)}, u32[]{:S(2)}, u32[]{:S(2)}) collective-permute-start(bf16[192,256]{1,0:T(8,128)(2,1)S(1)} %pad_maximum_fusion.8), channel_id=1, source_target_pairs={{0,4},{1,5},{2,6},{3,7},{4,0},{5,1},{6,2},{7,3},{8,12},{9,13},{10,... | collective-permute-start | bytes 294920 | tf_op jit(solution)/shard_map/ppermute | solution.py:181
  47.5 1.3 %collective-permute-start.11 = (bf16[64,256]{1,0:T(8,128)(2,1)S(1)}, bf16[64,256]{1,0:T(8,128)(2,1)S(1)}, u32[]{:S(2)}, u32[]{:S(2)}) collective-permute-start(bf16[64,256]{1,0:T(8,128)(2,1)S(1)} %add_convert_fusion.9), channel_id=1, source_target_pairs={{0,8},{8,0},{16,24},{24,16},{1,9},{9,1},{17,25},{25,17},{2,10},{10... | collective-permute-start | bytes 98312 | tf_op jit(solution)/shard_map/ppermute | solution.py:181
  47.6 25.2 %copy-start.3 = (f32[32,256]{1,0:T(8,128)S(1)}, f32[32,256]{1,0:T(8,128)}, u32[]{:S(2)}) copy-start(f32[32,256]{1,0:T(8,128)} %refs_3_.1) | copy-start | bytes 98308
  47.7 25.2 %copy-start.4 = (f32[32,256]{1,0:T(8,128)S(1)}, f32[32,256]{1,0:T(8,128)}, u32[]{:S(2)}) copy-start(f32[32,256]{1,0:T(8,128)} %refs_4_.1) | copy-start | bytes 98308
  47.7 25.2 %copy-start.5 = (f32[32,256]{1,0:T(8,128)S(1)}, f32[32,256]{1,0:T(8,128)}, u32[]{:S(2)}) copy-start(f32[32,256]{1,0:T(8,128)} %refs_5_.1) | copy-start | bytes 98308
  47.7 27.8 %copy-start.6 = (f32[16,256]{1,0:T(8,128)S(1)}, f32[16,256]{1,0:T(8,128)}, u32[]{:S(2)}) copy-start(f32[16,256]{1,0:T(8,128)} %refs_0_.1) | copy-start | bytes 49156
  47.7 27.8 %copy-start.7 = (f32[16,256]{1,0:T(8,128)S(1)}, f32[16,256]{1,0:T(8,128)}, u32[]{:S(2)}) copy-start(f32[16,256]{1,0:T(8,128)} %refs_1_.1) | copy-start | bytes 49156
  47.7 27.8 %copy-start.8 = (f32[16,256]{1,0:T(8,128)S(1)}, f32[16,256]{1,0:T(8,128)}, u32[]{:S(2)}) copy-start(f32[16,256]{1,0:T(8,128)} %refs_2_.1) | copy-start | bytes 49156
  59.0 1.3 %collective-permute-start.12 = (bf16[128,256]{1,0:T(8,128)(2,1)S(1)}, bf16[128,256]{1,0:T(8,128)(2,1)S(1)}, u32[]{:S(2)}, u32[]{:S(2)}) collective-permute-start(bf16[128,256]{1,0:T(8,128)(2,1)S(1)} %pad_maximum_fusion.10), channel_id=1, source_target_pairs={{0,8},{8,0},{16,24},{24,16},{1,9},{9,1},{17,25},{25,17},{2,10},{10... | collective-permute-start | bytes 196616 | tf_op jit(solution)/shard_map/ppermute | solution.py:181
  60.3 5.8 %collective-permute-start.15 = (bf16[64,256]{1,0:T(8,128)(2,1)S(1)}, bf16[64,256]{1,0:T(8,128)(2,1)S(1)}, u32[]{:S(2)}, u32[]{:S(2)}) collective-permute-start(bf16[64,256]{1,0:T(8,128)(2,1)S(1)} %add_convert_fusion.8), channel_id=1, source_target_pairs={{0,17},{1,16},{2,19},{3,18},{4,21},{5,20},{6,23},{7,22},{8,25},{9,... | collective-permute-start | bytes 98312 | tf_op jit(solution)/shard_map/ppermute | solution.py:205
  61.9 4.3 %collective-permute-start.13 = (bf16[128,256]{1,0:T(8,128)(2,1)S(1)}, bf16[128,256]{1,0:T(8,128)(2,1)S(1)}, u32[]{:S(2)}, u32[]{:S(2)}) collective-permute-start(bf16[128,256]{1,0:T(8,128)(2,1)S(1)} %pad_maximum_fusion.11), channel_id=1, source_target_pairs={{0,1},{1,0},{2,3},{3,2},{4,5},{5,4},{6,7},{7,6},{8,9},{9,8},{10,11... | collective-permute-start | bytes 196616 | tf_op jit(solution)/shard_map/ppermute | solution.py:181
  62.0 4.2 %collective-permute-start.14 = (bf16[96,256]{1,0:T(8,128)(2,1)S(1)}, bf16[96,256]{1,0:T(8,128)(2,1)S(1)}, u32[]{:S(2)}, u32[]{:S(2)}) collective-permute-start(bf16[96,256]{1,0:T(8,128)(2,1)S(1)} %pad_maximum_fusion.13), channel_id=1, source_target_pairs={{0,16},{8,24},{16,0},{24,8},{1,17},{9,25},{17,1},{25,9},{2,18},{10... | collective-permute-start | bytes 147464 | tf_op jit(solution)/shard_map/ppermute | solution.py:181
  66.2 4.2 %collective-permute-start.16 = (bf16[96,256]{1,0:T(8,128)(2,1)S(1)}, bf16[96,256]{1,0:T(8,128)(2,1)S(1)}, u32[]{:S(2)}, u32[]{:S(2)}) collective-permute-start(bf16[96,256]{1,0:T(8,128)(2,1)S(1)} %pad_maximum_fusion.14), channel_id=1, source_target_pairs={{0,2},{1,3},{2,0},{3,1},{4,6},{5,7},{6,4},{7,5},{8,10},{9,11},{10,... | collective-permute-start | bytes 147464 | tf_op jit(solution)/shard_map/ppermute | solution.py:181
  70.4 5.0 %collective-permute-start.17 = (bf16[80,256]{1,0:T(8,128)(2,1)S(1)}, bf16[80,256]{1,0:T(8,128)(2,1)S(1)}, u32[]{:S(2)}, u32[]{:S(2)}) collective-permute-start(bf16[80,256]{1,0:T(8,128)(2,1)S(1)} %pad_maximum_fusion.15), channel_id=1, source_target_pairs={{0,4},{1,5},{2,6},{3,7},{4,0},{5,1},{6,2},{7,3},{8,12},{9,13},{10,... | collective-permute-start | bytes 122888 | tf_op jit(solution)/shard_map/ppermute | solution.py:181
  75.4 1.3 %collective-permute-start.18 = (bf16[64,256]{1,0:T(8,128)(2,1)S(1)}, bf16[64,256]{1,0:T(8,128)(2,1)S(1)}, u32[]{:S(2)}, u32[]{:S(2)}) collective-permute-start(bf16[64,256]{1,0:T(8,128)(2,1)S(1)} %add_convert_fusion.5), channel_id=1, source_target_pairs={{0,8},{8,0},{16,24},{24,16},{1,9},{9,1},{17,25},{25,17},{2,10},{10... | collective-permute-start | bytes 98312 | tf_op jit(solution)/shard_map/ppermute | solution.py:181
